TPU v7x, 32 devices: a whole 2x2x4 slice. The times are simulated.
32 devices in a mesh: grp: 2 (over y), inp: 4 (over z), tblk: 2 (over x), sub: 2 (over core).
Axes of the slice: x: 2, y: 2, z: 4, core: 2. Of those that a mesh axis runs over, the one named last changes fastest.
Arguments:
- voltages: bfloat16 [1024, 393216], P(('grp', 'inp', 'sub'), 'tblk'), parts along dimension 0, may hold values from -6 to 6
- pfb_coeffs: float32 [16, 2048], replicated, may hold values from -1.5 to 1.5
- input_flags: int32 [1024, 192], P(('grp', 'inp', 'sub'), 'tblk'), parts along dimension 0, may hold values 0 or 1
- spec_good: int32 [384], P('grp'), parts along dimension 0, may hold values from 0 to 1, as said below
- chan_map: int32 [512], replicated, may hold values from 0 to 1023, as said below
Outputs:
- visibilities: bfloat16 [1024, 512, 512], P(('grp', 'inp', 'tblk', 'sub')), parts along dimension 0
There are 2 independent parts, one for each index of `grp`. A program takes and returns all parts, laid end to end along the dimension named above; an argument that names none is the same for every part. Nothing has to cross between parts.
Inputs may be any that keep to these rules, and one draw needn't show every extreme that they name: `spec_good`: in each aligned block of 96 spectra between 32 and 64 spectra are kept, and some block keeps exactly 64. `chan_map`: distinct channels; both 0 and 1023 appear.
All inputs are finite; a program needn't handle non-finite values. No bound on the sum of `input_flags` on one device may be relied on, other than what follows from the above.
Results may differ from a plain program's by a relative error of at most 0.0085.
Values may be sent and summed in bfloat16 or wider, within the bound.
No kernel may reach another device: no remote copies, remote signals or barrier semaphores. Data moves between devices by JAX's collectives and lax.ppermute only.
A program may use at most 192 MiB of HBM per device.

v0:
```python
import math

import jax
import jax.numpy as jnp
from jax import lax
from jax.sharding import PartitionSpec as P


def passed_along(value, axis, steps):
    count = lax.axis_size(axis)
    initial, last = (max(0, -steps), min(count, count - steps))
    return lax.ppermute(value, axis, [(source, source + steps) for source in range(initial, last)])


def make_table(channels, frame_len):
    samples = jnp.arange(frame_len, dtype=jnp.int32)
    phase_index = samples[:, None] * channels[None, :] % frame_len
    angles = phase_index.astype(jnp.float32) * (2.0 * math.pi / frame_len)
    norm_scale = 1.0 / math.sqrt(frame_len)
    return jnp.stack([jnp.cos(angles) * norm_scale, -jnp.sin(angles) * norm_scale], axis=1).astype(
        jnp.bfloat16
    )


def correlate_one(spectra_block):
    input_total = spectra_block.shape[0]
    half_width = spectra_block.shape[1] // 2
    rotated = jnp.concatenate(
        [spectra_block[:, half_width:], -spectra_block[:, :half_width]], axis=1
    )
    stacked = jnp.concatenate([spectra_block, rotated], axis=0)
    products = jnp.dot(stacked, spectra_block.T, preferred_element_type=jnp.float32)
    upper_mask = jnp.arange(input_total)[None, :] >= jnp.arange(input_total)[:, None]
    return jnp.where(upper_mask, products[:input_total], products[input_total:])


def rounded(values):
    return lax.optimization_barrier(values.astype(jnp.bfloat16)).astype(jnp.float32)


def local(voltages, pfb_coeffs, input_flags, spec_good, chan_map):
    tap_count, frame_len = pfb_coeffs.shape
    local_inputs, block_len = input_flags.shape
    frames = voltages.reshape(local_inputs, block_len, frame_len)
    earlier = passed_along(frames[:, block_len - tap_count + 1 :, :], "tblk", 1)
    extended = jnp.concatenate([earlier, frames], axis=1)
    summed = jnp.zeros((local_inputs, block_len, frame_len), jnp.float32)
    for tap_index in range(tap_count):
        window_part = extended[:, tap_index : tap_index + block_len, :]
        summed = summed + pfb_coeffs[tap_index][None, None, :] * window_part.astype(jnp.float32)
    block_index = lax.axis_index("tblk")
    good_here = lax.dynamic_slice_in_dim(spec_good, block_index * block_len, block_len)
    weights = input_flags * good_here[None, :]
    filtered = (summed * weights.astype(jnp.float32)[:, :, None]).astype(jnp.bfloat16)
    inp_count = lax.axis_size("inp")
    tblk_count = lax.axis_size("tblk")
    sub_count = lax.axis_size("sub")
    chan_total = chan_map.shape[0]
    per_owner = chan_total // (inp_count * tblk_count * sub_count)
    live_total = jnp.sum(spec_good).astype(jnp.float32)
    slot_order = jnp.arange(chan_total).reshape(inp_count, tblk_count, sub_count, per_owner)
    slot_order = slot_order.transpose(0, 2, 1, 3).reshape(chan_total)
    dft_table = make_table(chan_map[slot_order], frame_len)
    spectra = jnp.einsum("isn,nqj->jiqs", filtered, dft_table, preferred_element_type=jnp.float32)
    spectra = spectra.astype(jnp.bfloat16).reshape(chan_total, local_inputs, -1)
    turned = lax.all_to_all(spectra, ("inp", "sub"), split_axis=0, concat_axis=1, tiled=True)
    summed_vis = lax.psum_scatter(
        rounded(lax.map(correlate_one, turned)).astype(jnp.bfloat16),
        "tblk",
        scatter_dimension=0,
        tiled=True,
    ).astype(jnp.float32)
    return (summed_vis / live_total).astype(jnp.bfloat16)


def solution(mesh):
    return jax.shard_map(
        local,
        mesh=mesh,
        in_specs=(
            P(("grp", "inp", "sub"), "tblk"),
            P(),
            P(("grp", "inp", "sub"), "tblk"),
            P("grp"),
            P(),
        ),
        out_specs=P(("grp", "inp", "tblk", "sub"), None, None),
        check_vma=False,
    )
```

profile of v0, /device:TPU:0, one launch (start us, length us, event | category | flops | bytes accessed | tf_op | source)
XLA Modules:
  0.0 1400.0 jit_solution(2505238213675392294)
XLA Ops:
  6.5 21.9 %copy.22 = bf16[8,8,96,2048]{3,2,1,0:T(8,128)(2,1)S(1)} copy(bf16[8,8,96,2048]{3,1,2,0:T(8,128)(2,1)} %bitcast.62) | data formatting | bytes 50331648
  28.5 8.3 copy-done.2
  36.7 1.9 slice.146
  38.7 4.2 copy.16
  42.9 6.7 collective-permute-start
  49.8 3.5 gather_fusion
  53.4 17.1 %multiply_convert_fusion.3 = (bf16[2048,1,512]{2,0,1:T(8,128)(2,1)S(1)}, bf16[2048,1,512]{2,0,1:T(8,128)(2,1)S(1)}) fusion(s32[512]{0:T(512)S(1)} %gather_fusion), kind=kLoop, calls=%fused_computation.70 | loop fusion | flops 19922944 | bytes 4196352 | tf_op jit(solution)/shard_map/convert
  70.6 61.7 %collective-permute-done = bf16[64,15,2048]{2,0,1:T(8,128)(2,1)} collective-permute-done((bf16[64,15,2048]{2,0,1:T(8,128)(2,1)}, bf16[64,15,2048]{2,0,1:T(8,128)(2,1)}, u32[]{:S(2)}, u32[]{:S(2)}) %collective-permute-start) | collective-permute-done | bytes 3932192 | tf_op jit(solution)/shard_map/ppermute | solution.py:12
  132.2 4.3 copy.17
  136.5 266.2 %fusion.42 = bf16[64,96,2048,1]{2,1,0,3:T(8,128)(2,1)} fusion(f32[64,96]{1,0:T(8,128)S(1)} %multiply_convert_fusion.4, bf16[64,96,2048]{2,1,0:T(8,128)(2,1)} %bitcast.60, f32[2048]{0:T(1024)S(1)} %bitcast.78, bf16[64,15,2048]{2,1,0:T(8,128)(2,1)S(1)} %copy.17, f32[2048]{0:T(1024)S(1)} %bitcast.79, f32[2048]{0:T(1024)S(1)} %bitcast.65, ...), kind=kLoop, calls=%fused_computation.58.clone.clone.clone.2 | loop fusion | flops 1182793728 | bytes 54419456 | tf_op jit(solution)/shard_map/isn,nqj->jiqs/dot_general | solution.py:64
  402.7 31.4 %convert_bitcast_fusion = bf16[512,64,2,96]{0,3,1,2:T(8,128)(2,1)} fusion(bf16[2048,1,512]{2,0,1:T(8,128)(2,1)S(1)} %get-tuple-element.48, bf16[2048,1,512]{2,0,1:T(8,128)(2,1)S(1)} %get-tuple-element.47, bf16[64,96,2048,1]{2,1,0,3:T(8,128)(2,1)} %fusion.42), kind=kOutput, calls=%fused_computation.59 | convolution fusion | flops 25784483840 | bytes 41943040 | tf_op jit(solution)/shard_map/isn,nqj->jiqs/dot_general | solution.py:64
  434.1 10.8 copy.18
  444.9 24.3 %copy.19 = bf16[512,64,192]{2,1,0:T(8,128)(2,1)} copy(bf16[512,64,192]{0,2,1:T(8,128)(2,1)} %bitcast.61) | data formatting | bytes 25165824 | tf_op jit(solution)/shard_map/reshape | solution.py:65
  469.3 5.7 all-to-all-start
  475.1 363.6 %all-to-all-done = bf16[512,64,192]{2,1,0:T(8,128)(2,1)} async-done(((bf16[512,64,192]{2,1,0:T(8,128)(2,1)}), bf16[512,64,192]{2,1,0:T(8,128)(2,1)}, u32[]{:S(2)}, u32[]{:S(2)}) %all-to-all-start) | async-done | bytes 12582944 | tf_op jit(solution)/shard_map/all_to_all | solution.py:66
  838.7 14.2 %copy.20 = bf16[64,8,64,192]{3,2,1,0:T(8,128)(2,1)} copy(bf16[64,8,64,192]{3,2,0,1:T(8,128)(2,1)} %bitcast.25) | data formatting | bytes 25165824 | tf_op jit(solution)/shard_map/all_to_all | solution.py:66
  852.8 156.7 %while.10 = (s32[]{:T(128)}, bf16[64,512,512]{2,1,0:T(8,128)(2,1)}, bf16[64,512,192]{2,1,0:T(8,128)(2,1)}, s32[]{:T(128)}) while((s32[]{:T(128)}, bf16[64,512,512]{2,1,0:T(8,128)(2,1)}, bf16[64,512,192]{2,1,0:T(8,128)(2,1)}, s32[]{:T(128)}) %tuple.42), condition=%wide.region_1.2_spmd, body=%wide.region_0.0_spmd.sunk | while | flops 203079680 | bytes 3801657 | solution.py:68
  852.8 1.0 dynamic-slice_bitcast_fusion.2
  855.3 1.0 dynamic-slice_bitcast_fusion.2
  857.7 1.0 dynamic-slice_bitcast_fusion.2
  860.2 1.0 dynamic-slice_bitcast_fusion.2
  862.6 1.0 dynamic-slice_bitcast_fusion.2
  865.0 1.0 dynamic-slice_bitcast_fusion.2
  867.5 1.0 dynamic-slice_bitcast_fusion.2
  869.9 1.0 dynamic-slice_bitcast_fusion.2
  872.3 1.0 dynamic-slice_bitcast_fusion.2
  874.8 1.0 dynamic-slice_bitcast_fusion.2
  877.2 1.0 dynamic-slice_bitcast_fusion.2
  919.0 1.0 dynamic-slice_bitcast_fusion.2
  975.3 1.0 dynamic-slice_bitcast_fusion.2
  1010.8 367.7 %reduce-scatter.2.cloned.1.call-done = bf16[32,512,512]{2,1,0:T(8,128)(2,1)} async-done(((bf16[64,512,512]{2,1,0:T(8,128)(2,1)}), bf16[32,512,512]{2,1,0:T(8,128)(2,1)}) %reduce-scatter.2.cloned.1.call-update) | async-done | bytes 16777232 | tf_op jit(solution)/shard_map/reduce_scatter | solution.py:67
  1378.5 14.7 %divide_convert_fusion = bf16[32,512,512]{2,1,0:T(8,128)(2,1)} fusion(bf16[32,512,512]{2,1,0:T(8,128)(2,1)} %reduce-scatter.2.cloned.1.call-done, f32[]{:T(128)S(6)} %convert_element_type.112), kind=kLoop, calls=%fused_computation.29 | loop fusion | flops 25165824 | bytes 33554436 | tf_op jit(solution)/shard_map/convert_element_type | solution.py:73
  (265 shorter events, 144.3 us)
Async XLA Ops:
  6.5 43.2 %copy-start = (s32[512]{0:T(512)S(1)}, s32[512]{0:T(512)}, u32[]{:S(2)}) copy-start(s32[512]{0:T(512)} %param.11) | copy-start | bytes 6148
  6.5 43.1 %copy-start.5 = (s32[192]{0:T(256)S(1)}, s32[192]{0:T(256)}, u32[]{:S(2)}) copy-start(s32[192]{0:T(256)} %param.10) | copy-start | bytes 2308
  6.5 46.8 %copy-start.4 = (s32[64,96]{1,0:T(8,128)S(1)}, s32[64,96]{1,0:T(8,128)}, u32[]{:S(2)}) copy-start(s32[64,96]{1,0:T(8,128)} %param.9) | copy-start | bytes 73732
  6.5 46.8 %copy-start.3 = (f32[16,2048]{1,0:T(8,128)S(1)}, f32[16,2048]{1,0:T(8,128)}, u32[]{:S(2)}) copy-start(f32[16,2048]{1,0:T(8,128)} %param.8) | copy-start | bytes 393220
  28.4 8.3 copy-start.2
  42.9 89.3 %collective-permute-start = (bf16[64,15,2048]{2,0,1:T(8,128)(2,1)}, bf16[64,15,2048]{2,0,1:T(8,128)(2,1)}, u32[]{:S(2)}, u32[]{:S(2)}) collective-permute-start(bf16[64,15,2048]{2,0,1:T(8,128)(2,1)} %copy.16), channel_id=1, source_target_pairs={{0,2},{1,3},{4,6},{5,7},{8,10},{9,11},{12,14},{13,15},{16,18},{17,... | collective-permute-start | bytes 11796488 | tf_op jit(solution)/shard_map/ppermute | solution.py:12
  469.3 369.4 %all-to-all-start = ((bf16[512,64,192]{2,1,0:T(8,128)(2,1)}), bf16[512,64,192]{2,1,0:T(8,128)(2,1)}, u32[]{:S(2)}, u32[]{:S(2)}) async-start(bf16[512,64,192]{2,1,0:T(8,128)(2,1)} %copy.19), calls=%async_computation | async-start | bytes 33554432 | tf_op jit(solution)/shard_map/all_to_all | solution.py:66
  475.0 903.4 %reduce-scatter.2.cloned.1.call-start = ((), (), s32[]{:S(2)}) async-start(), calls=%async_computation.2 | async-start | bytes 50331648 | tf_op jit(solution)/shard_map/reduce_scatter | solution.py:67
  1009.5 383.7 %copy-start.1 = (s32[512]{0:T(512)S(1)}, s32[512]{0:T(512)}, u32[]{:S(2)}) copy-start(s32[512]{0:T(512)} %param.11) | copy-start | bytes 6148
Sparse Core Ops, SparseCore 0:
  1009.6 368.7 reduce-scatter.1
where the time goes:
time: 1400 us
  waiting for transfers between devices  793 us (57%)
  other arithmetic  362 us (26%)
  local copies, waits for them, and re-layouts  156 us (11%)
  matrix products  62.3 us (4%)
  between operations  14.2 us (1%)
    reduce_scatter x1, waiting for transfers between devices, local(): lax.psum_scatter(rounded(lax.map(correlate_one, turned)).astype(jnp.bfloa...  368 us
    all_to_all x1, waiting for transfers between devices, local(): lax.all_to_all(spectra, ('inp', 'sub'), split_axis=0, concat_axis=1, tile...  364 us
    dot_general x1, other arithmetic, local(): jnp.einsum('isn,nqj->jiqs', filtered, dft_table, preferred_element_type=j...  266 us
    squeeze x64, local copies, waits for them, and re-layouts, local(): lax.map(correlate_one, turned)  61.9 us
    ppermute x1, waiting for transfers between devices, passed_along(): lax.ppermute(value, axis, [(source, source + steps) for source in range(i...  61.7 us
    dynamic_update_slice x64, other arithmetic, local(): lax.map(correlate_one, turned)  56.2 us
    dot_general x1, matrix products, local(): jnp.einsum('isn,nqj->jiqs', filtered, dft_table, preferred_element_type=j...  31.4 us
    dot_general x64, matrix products, correlate_one(): jnp.dot(stacked, spectra_block.T, preferred_element_type=jnp.float32)  30.9 us
  transfers between devices with their start and end apart: 3, of which 3 were waited for; matrix products, arithmetic and copies ran while one was open for 2% of the time, Pallas kernels for 0%

commit v1 on v0

--- a/solution.py
+++ b/solution.py
@@ -1,9 +1,18 @@
+import functools
 import math
 
 import jax
 import jax.numpy as jnp
 from jax import lax
+from jax.experimental import pallas as pl
+from jax.experimental.pallas import tpu as pltpu
 from jax.sharding import PartitionSpec as P
+
+MAX_KEPT = 64
+STEP = 16
+LANES = 128
+COLS = 256
+VMEM_BYTES = 56 * 1024 * 1024
 
 
 def passed_along(value, axis, steps):
@@ -13,6 +22,233 @@
 
 
 def make_table(channels, frame_len):
+    scale = 2.0 * math.pi / frame_len
+    fine = jnp.arange(LANES, dtype=jnp.int32)
+    coarse = jnp.arange(frame_len // LANES, dtype=jnp.int32) * LANES
+    fine_angle = (channels[:, None] * fine[None, :] % frame_len).astype(jnp.float32) * scale
+    coarse_angle = (channels[:, None] * coarse[None, :] % frame_len).astype(jnp.float32) * scale
+    norm_scale = 1.0 / math.sqrt(frame_len)
+    parts = (jnp.cos(fine_angle), jnp.sin(fine_angle), jnp.cos(coarse_angle) * norm_scale, jnp.sin(coarse_angle) * norm_scale)
+    fine_cos, fine_sin, coarse_cos, coarse_sin = lax.optimization_barrier(parts)
+    fine_cos, fine_sin = fine_cos[:, None, :], fine_sin[:, None, :]
+    coarse_cos, coarse_sin = coarse_cos[:, :, None], coarse_sin[:, :, None]
+    cosine = coarse_cos * fine_cos - coarse_sin * fine_sin
+    sine = coarse_sin * fine_cos + coarse_cos * fine_sin
+    table = jnp.stack([cosine, -sine]).astype(jnp.bfloat16)
+    return table.reshape(2 * channels.shape[0], frame_len)
+
+
+def kept_rows(good, most):
+    length = good.shape[0]
+    place = jnp.arange(length, dtype=jnp.int32)
+    before = jnp.sum(jnp.where(place[:, None] <= place[None, :], good[:, None], 0), axis=0)
+    row = jnp.arange(most, dtype=jnp.int32)
+    index = jnp.sum((before[None, :] <= row[:, None]).astype(jnp.int32), axis=1)
+    index = jnp.minimum(index, length - 1)
+    used = row < jnp.sum(good)
+    chosen = (place[None, :] == index[:, None]) & used[:, None]
+    return index, chosen
+
+
+def transform_kernel(slots, with_halo, index_ref, volt_ref, halo_ref, coef_ref, table_ref, weight_ref, out_ref, raw, wide, filt, turn, sems):
+    taps, frame_len = coef_ref.shape
+    ins = filt.shape[0] // STEP
+    first = index_ref[0]
+    count = index_ref[STEP - 1] - first + taps
+
+    def each(col, slot, act):
+        def body(j, carry):
+            extended = first + j
+            if with_halo:
+
+                @pl.when(extended < taps - 1)
+                def _():
+                    begin = pl.multiple_of(extended * frame_len + col * COLS, COLS)
+                    act(pltpu.make_async_copy(halo_ref.at[:, pl.ds(begin, COLS)], raw.at[slot, j], sems.at[slot, j]))
+
+            @pl.when(extended >= taps - 1)
+            def _():
+                begin = pl.multiple_of((extended - (taps - 1)) * frame_len + col * COLS, COLS)
+                act(pltpu.make_async_copy(volt_ref.at[:, pl.ds(begin, COLS)], raw.at[slot, j], sems.at[slot, j]))
+
+            return carry
+
+        lax.fori_loop(0, count, body, 0)
+
+    cols = frame_len // COLS
+    each(0, 0, lambda c: c.start())
+
+    def column(col, carry):
+        slot = lax.rem(col, 2)
+
+        @pl.when(col + 1 < cols)
+        def _():
+            each(col + 1, 1 - slot, lambda c: c.start())
+
+        each(col, slot, lambda c: c.wait())
+
+        def widen(j, inner):
+            wide[j] = raw[slot, j].astype(jnp.float32)
+            return inner
+
+        lax.fori_loop(0, count, widen, 0)
+        for half in range(COLS // LANES):
+            span = pl.ds(half * LANES, LANES)
+            here = pl.ds(pl.multiple_of(col * COLS + half * LANES, LANES), LANES)
+            coefs = [jnp.broadcast_to(coef_ref[pl.ds(k, 1), here], (8, LANES)) for k in range(taps)]
+
+            def one(r, inner):
+                base = index_ref[r] - first
+                for group in range(ins // 16):
+                    rows = pl.ds(group * 16, 16)
+                    total = None
+                    for k in range(taps):
+                        term = wide[base + k, rows, span].reshape(2, 8, LANES) * coefs[k][None]
+                        total = term if total is None else total + term
+                    at = pl.ds(pl.multiple_of(r * ins + group * 16, 16), 16)
+                    filt[at, here] = total.reshape(16, LANES).astype(jnp.bfloat16)
+                return inner
+
+            lax.fori_loop(0, STEP, one, 0)
+        return carry
+
+    lax.fori_loop(0, cols, column, 0)
+
+    pairs = STEP * ins // LANES
+    per_dot = COLS // LANES
+
+    def multiply(m, carry):
+        rows = pl.ds(pl.multiple_of(m * COLS, COLS), COLS)
+        for n in range(pairs // per_dot):
+            spec = lax.dot_general(
+                table_ref[rows, :],
+                filt[pl.ds(n * COLS, COLS), :],
+                (((1,), (1,)), ((), ())),
+                preferred_element_type=jnp.float32,
+            )
+            for h in range(per_dot):
+                b = n * per_dot + h
+                turn[pl.ds(pl.multiple_of(b * 2 * slots + m * COLS, COLS), COLS), :] = (
+                    spec[:, h * LANES : (h + 1) * LANES] * weight_ref[pl.ds(b, 1), :]
+                )
+        return carry
+
+    lax.fori_loop(0, 2 * slots // COLS, multiply, 0)
+
+    def corner(j, carry):
+        for u in range(8):
+            slot = j * 8 + u
+            real = turn[pl.ds(slot, pairs, stride=2 * slots), :]
+            imag = turn[pl.ds(slots + slot, pairs, stride=2 * slots), :]
+            out_ref[slot] = jnp.concatenate([real, imag], axis=0).astype(jnp.bfloat16)
+        return carry
+
+    lax.fori_loop(0, slots // 8, corner, 0)
+
+
+def transform(voltages, halo, coefs, table, index, weight, with_halo):
+    ins = voltages.shape[0]
+    taps, frame_len = coefs.shape
+    slots = table.shape[0] // 2
+    frames = voltages.shape[1] // frame_len + taps - 1
+    pairs = STEP * ins // LANES
+    flops = 2 * STEP * ins * frame_len * 2 * slots
+    vmem = pl.BlockSpec(memory_space=pltpu.VMEM)
+    hbm = pl.BlockSpec(memory_space=pl.ANY)
+    return pl.pallas_call(
+        functools.partial(transform_kernel, slots, with_halo),
+        out_shape=jax.ShapeDtypeStruct((slots, 2 * pairs, LANES), jnp.bfloat16),
+        in_specs=[pl.BlockSpec(memory_space=pltpu.SMEM), hbm, hbm, vmem, vmem, vmem],
+        out_specs=vmem,
+        scratch_shapes=[
+            pltpu.VMEM((2, frames, ins, COLS), jnp.bfloat16),
+            pltpu.VMEM((frames, ins, COLS), jnp.float32),
+            pltpu.VMEM((STEP * ins, frame_len), jnp.bfloat16),
+            pltpu.VMEM((pairs * 2 * slots, LANES), jnp.float32),
+            pltpu.SemaphoreType.DMA((2, frames)),
+        ],
+        compiler_params=pltpu.CompilerParams(vmem_limit_bytes=VMEM_BYTES),
+        cost_estimate=pl.CostEstimate(flops=4 * flops, bytes_accessed=12 * 2**20, transcendentals=0),
+        name="filter_transform",
+    )(index, voltages, halo, coefs, table, weight)
+
+
+def correlate_kernel(blocks, chips, cores, pieces, *refs):
+    scale_ref, refs = refs[0], refs[1:]
+    part_refs = refs[:pieces]
+    out_ref, straight, turned = refs[-3:]
+    ins = LANES // cores
+    total = straight.shape[1]
+    half_depth = part_refs[0].shape[-2] // 2
+    low = lax.broadcasted_iota(jnp.int32, (half_depth, LANES), 1) < ins
+    for chip in range(chips):
+        lanes = pl.ds(chip * LANES, LANES)
+        place = 0
+        for block in range(blocks):
+            sources = [(chip * blocks + block) * cores + core for core in range(cores)]
+            for part in part_refs:
+                for step in range(part.shape[1]):
+                    one, two = (part[source, step, 0].astype(jnp.float32) for source in sources)
+                    one = (one[:half_depth], one[half_depth:])
+                    two = (two[:half_depth], two[half_depth:])
+                    first = [jnp.where(low, a, pltpu.roll(b, ins, 1)) for a, b in zip(one, two)]
+                    second = [jnp.where(low, pltpu.roll(a, ins, 1), b) for a, b in zip(one, two)]
+                    for real, imag in (first, second):
+                        rows = pl.ds(place, 2 * half_depth)
+                        straight[rows, lanes] = jnp.concatenate([real, imag], axis=0).astype(jnp.bfloat16)
+                        turned[rows, lanes] = jnp.concatenate([-imag, real], axis=0).astype(jnp.bfloat16)
+                        place += 2 * half_depth
+    left = straight[...].T
+    scale = scale_ref[0]
+    half = total // 2
+
+    def product(a, ref, b):
+        return jnp.dot(left[a * half : (a + 1) * half], ref[:, b * half : (b + 1) * half], preferred_element_type=jnp.float32) * scale
+
+    upper = lax.broadcasted_iota(jnp.int32, (half, half), 1) >= lax.broadcasted_iota(jnp.int32, (half, half), 0)
+    for a in range(2):
+        here = pl.ds(a * half, half)
+        both = jnp.where(upper, product(a, straight, a), product(a, turned, a))
+        out_ref[0, here, here] = both.astype(out_ref.dtype)
+    out_ref[0, :half, half:] = product(0, straight, 1).astype(out_ref.dtype)
+    out_ref[0, half:, :half] = product(1, turned, 0).astype(out_ref.dtype)
+
+
+def correlate(scale, parts, into, first, own, blocks, chips, cores):
+    count = min(part.shape[2] - begin for part, begin in parts)
+    sources = blocks * chips * cores
+    total = chips * LANES
+    depth = blocks * cores * sum(part.shape[1] * part.shape[3] for part, _ in parts)
+
+    def spec(part, begin):
+        return pl.BlockSpec((sources, part.shape[1], 1) + part.shape[3:], lambda c: (0, 0, c + begin, 0, 0))
+
+    arrays = [part for part, _ in parts]
+    in_specs = [pl.BlockSpec(memory_space=pltpu.SMEM)] + [spec(*pair) for pair in parts]
+    operands = [scale] + arrays
+    aliases = {}
+    kernel = functools.partial(correlate_kernel, blocks, chips, cores, len(parts))
+    if into is not None:
+        aliases = {len(operands): 0}
+        operands.append(into)
+        in_specs.append(pl.BlockSpec(memory_space=pl.ANY))
+    return pl.pallas_call(
+        kernel,
+        grid=(count,),
+        out_shape=jax.ShapeDtypeStruct((own, total, total), jnp.bfloat16),
+        in_specs=in_specs,
+        out_specs=pl.BlockSpec((1, total, total), lambda c: (c + first, 0, 0)),
+        scratch_shapes=[pltpu.VMEM((depth, total), jnp.bfloat16)] * 2,
+        input_output_aliases=aliases,
+        compiler_params=pltpu.CompilerParams(vmem_limit_bytes=VMEM_BYTES),
+        cost_estimate=pl.CostEstimate(
+            flops=count * 8 * total * total * depth, bytes_accessed=count * 3 * total * total, transcendentals=0
+        ),
+        name="correlate",
+    )(*operands)
+
+
+def make_plain_table(channels, frame_len):
     samples = jnp.arange(frame_len, dtype=jnp.int32)
     phase_index = samples[:, None] * channels[None, :] % frame_len
     angles = phase_index.astype(jnp.float32) * (2.0 * math.pi / frame_len)
@@ -38,7 +274,7 @@
     return lax.optimization_barrier(values.astype(jnp.bfloat16)).astype(jnp.float32)
 
 
-def local(voltages, pfb_coeffs, input_flags, spec_good, chan_map):
+def local_plain(voltages, pfb_coeffs, input_flags, spec_good, chan_map):
     tap_count, frame_len = pfb_coeffs.shape
     local_inputs, block_len = input_flags.shape
     frames = voltages.reshape(local_inputs, block_len, frame_len)
@@ -60,7 +296,7 @@
     live_total = jnp.sum(spec_good).astype(jnp.float32)
     slot_order = jnp.arange(chan_total).reshape(inp_count, tblk_count, sub_count, per_owner)
     slot_order = slot_order.transpose(0, 2, 1, 3).reshape(chan_total)
-    dft_table = make_table(chan_map[slot_order], frame_len)
+    dft_table = make_plain_table(chan_map[slot_order], frame_len)
     spectra = jnp.einsum("isn,nqj->jiqs", filtered, dft_table, preferred_element_type=jnp.float32)
     spectra = spectra.astype(jnp.bfloat16).reshape(chan_total, local_inputs, -1)
     turned = lax.all_to_all(spectra, ("inp", "sub"), split_axis=0, concat_axis=1, tiled=True)
@@ -71,6 +307,54 @@
         tiled=True,
     ).astype(jnp.float32)
     return (summed_vis / live_total).astype(jnp.bfloat16)
+
+
+def local(voltages, pfb_coeffs, input_flags, spec_good, chan_map):
+    taps, frame_len = pfb_coeffs.shape
+    ins, block_len = input_flags.shape
+    chips, blocks, cores = (lax.axis_size(axis) for axis in ("inp", "tblk", "sub"))
+    owners = chips * blocks * cores
+    slots = chan_map.shape[0]
+    own = slots // owners
+    if ins * cores != LANES or own % 2 or ins % 16:
+        return local_plain(voltages, pfb_coeffs, input_flags, spec_good, chan_map)
+    halo = passed_along(voltages[:, (block_len - taps + 1) * frame_len :], "tblk", 1)
+    good = lax.dynamic_slice_in_dim(spec_good, lax.axis_index("tblk") * block_len, block_len)
+    index, chosen = kept_rows(good, MAX_KEPT)
+    weight = jnp.dot(
+        chosen.astype(jnp.bfloat16), input_flags.astype(jnp.bfloat16).T, preferred_element_type=jnp.float32
+    ).reshape(MAX_KEPT * ins // LANES, LANES)
+    table = make_table(chan_map, frame_len)
+    pairs = STEP * ins // LANES
+    scale = (1.0 / jnp.sum(spec_good).astype(jnp.float32)).reshape(1)
+
+    def chunk(step):
+        done = transform(
+            voltages,
+            halo if step == 0 else voltages,
+            pfb_coeffs,
+            table,
+            index[step * STEP : (step + 1) * STEP],
+            weight[step * pairs : (step + 1) * pairs],
+            step == 0,
+        )
+        return done.reshape(owners, 1, own, 2 * pairs, LANES)
+
+    def turn(piece):
+        return lax.all_to_all(piece, ("inp", "tblk", "sub"), split_axis=0, concat_axis=0, tiled=True)
+
+    early = turn(chunk(1))
+    middle = turn(jnp.concatenate([chunk(2), chunk(3)], axis=1))
+    last = chunk(0)
+    cuts = 2
+    each = own // cuts
+    out = None
+    for cut in range(cuts):
+        tail = turn(last[:, :, cut * each : (cut + 1) * each])
+        out = correlate(
+            scale, [(early, cut * each), (middle, cut * each), (tail, 0)], out, cut * each, own, blocks, chips, cores
+        )
+    return out
 
 
 def solution(mesh):

time: 1400 us -> 378 us (0.27)
  waiting for transfers between devices: 793 us -> 40.1 us
  other arithmetic: 362 us -> 13.3 us
  Pallas kernels: 0 us -> 172 us
  local copies, waits for them, and re-layouts: 156 us -> 18.3 us
  blocking collectives: 0 us -> 107 us
  matrix products: 62.3 us -> 0.2 us
    reduce_scatter x1 -> x0, waiting for transfers between devices: 368 us -> none  [local(): lax.psum_scatter(rounded(lax.map(correlate_one, turned)).astype(jnp.bfloa...]
    all_to_all x1 -> x3, waiting for transfers between devices: 364 us -> 6.62 us  [turn(): lax.all_to_all(piece, ('inp', 'tblk', 'sub'), split_axis=0, concat_axis=0...]
    dot_general x1 -> x0, other arithmetic: 266 us -> none  [local(): jnp.einsum('isn,nqj->jiqs', filtered, dft_table, preferred_element_type=j...]
    pallas_call x0 -> x6, Pallas kernels: none -> 172 us  [the longest x4 142 us: transform(): pl.pallas_call(functools.partial(transform_kernel, slots, with_halo), out...]
    all_to_all x0 -> x1, blocking collectives: none -> 107 us  [turn(): lax.all_to_all(piece, ('inp', 'tblk', 'sub'), split_axis=0, concat_axis=0...]
    dot_general x65 -> x1, matrix products: 62.3 us -> 0.2 us  [local(): jnp.dot(chosen.astype(jnp.bfloat16), input_flags.astype(jnp.bfloat16).T,...]
    squeeze x64 -> x0, local copies, waits for them, and re-layouts: 61.9 us -> none  [local(): lax.map(correlate_one, turned)]
    dynamic_update_slice x64 -> x0, other arithmetic: 56.2 us -> none  [local(): lax.map(correlate_one, turned)]
  transfers between devices with their start and end apart: 3 -> 4, of which waited for: 3 -> 2; matrix products, arithmetic and copies ran while one was open for 2% -> 7% of each run, Pallas kernels for 0% -> 42%
where the time goes in v1:
time: 378 us; the launch traced here: 373 us
  Pallas kernels  172 us (46%)
  blocking collectives  107 us (28%)
  waiting for transfers between devices  40.1 us (11%)
  starting transfers between devices  20.7 us (5%)
  local copies, waits for them, and re-layouts  18.3 us (5%)
  other arithmetic  13.3 us (4%)
    pallas_call x4, Pallas kernels, transform(): pl.pallas_call(functools.partial(transform_kernel, slots, with_halo), out...  142 us
    all_to_all x1, blocking collectives, turn(): lax.all_to_all(piece, ('inp', 'tblk', 'sub'), split_axis=0, concat_axis=0...  107 us
    ppermute x1, waiting for transfers between devices, passed_along(): lax.ppermute(value, axis, [(source, source + steps) for source in range(i...  33.5 us
    pallas_call x2, Pallas kernels, correlate(): pl.pallas_call(kernel, grid=(count,), out_shape=jax.ShapeDtypeStruct((own...  30 us
    all_to_all x3, starting transfers between devices, turn(): lax.all_to_all(piece, ('inp', 'tblk', 'sub'), split_axis=0, concat_axis=0...  14 us
  transfers between devices with their start and end apart: 4, of which 2 were waited for; matrix products, arithmetic and copies ran while one was open for 7% of the time, Pallas kernels for 42%

profile of v1, /device:TPU:0, one launch (start us, length us, event | category | flops | bytes accessed | tf_op | source)
XLA Modules:
  0.0 373.0 jit_solution(1362998308996327477)
XLA Ops:
  0.0 4.3 %slice.55 = bf16[64,30720]{1,0:T(8,128)(2,1)} slice(bf16[64,196608]{1,0:T(8,128)(2,1)} %volt_ref.7), slice={[0:64], [165888:196608]} | slice | bytes 7864320 | tf_op jit(solution)/shard_map/slice | solution.py:321
  4.3 6.7 %collective-permute-start = (bf16[64,30720]{1,0:T(8,128)(2,1)}, bf16[64,30720]{1,0:T(8,128)(2,1)}, u32[]{:S(2)}, u32[]{:S(2)}) collective-permute-start(bf16[64,30720]{1,0:T(8,128)(2,1)} %slice.55), channel_id=1, source_target_pairs={{0,2},{1,3},{4,6},{5,7},{8,10},{9,11},{12,14},{13,15},{16,18},{17,... | collective-permute-start | bytes 11796488 | tf_op jit(solution)/shard_map/ppermute | solution.py:21
  11.1 0.7 fusion.17
  11.9 0.1 convert_reduce_fusion
  12.0 0.7 iota_compare_fusion.3
  12.7 0.2 fusion.12
  12.9 1.1 fusion.9
  14.0 1.1 sine_multiply_fusion
  15.1 2.5 subtract_convert_fusion
  17.6 2.4 pad_maximum_fusion
  19.9 0.7 slice.47.weight_ref
  20.6 6.3 %copy.9 = bf16[128,8,16,128]{3,1,2,0:T(8,128)(2,1)} copy(bf16[128,8,16,128]{3,2,1,0:T(8,128)(2,1)} %bitcast.10) | data formatting | bytes 8388608
  26.9 0.7 fusion.20
  27.5 41.5 %filter_transform.4 = bf16[512,16,128]{2,1,0:T(8,128)(2,1)} custom-call(s32[16]{0:T(128)} %get-tuple-element.30.index_ref, bf16[64,196608]{1,0:T(8,128)(2,1)} %volt_ref.7, bf16[64,196608]{1,0:T(8,128)(2,1)} %volt_ref.7, f32[16,2048]{1,0:T(8,128)} %coef_ref.7, bf16[1024,2048]{1,0:T(8,128)(2,1)} %bitcast.11, f32[8,128]{1,0:T(8,128)} %slice.47.weight_ref), custom_call_target="tpu_custom_call" | custom-call | flops 17179869184 | bytes 12582912 | tf_op jit(solution)/shard_map/filter_transform/pallas_call | solution.py:158
  69.1 5.0 %all-to-all-start = ((bf16[16,1,32,16,128]{4,3,2,1,0:T(8,128)(2,1)}), bf16[16,1,32,16,128]{4,3,2,1,0:T(8,128)(2,1)S(1)}, u32[]{:S(2)}, u32[]{:S(2)}) async-start(bf16[16,1,32,16,128]{4,3,2,1,0:T(8,128)(2,1)} %bitcast.15), calls=%async_computation | async-start | bytes 4194304 | tf_op jit(solution)/shard_map/all_to_all | solution.py:344
  74.1 0.7 slice.57.weight_ref
  74.7 0.7 slice.53.weight_ref
  75.4 33.5 %collective-permute-done.halo_ref = bf16[64,30720]{1,0:T(8,128)(2,1)} collective-permute-done((bf16[64,30720]{1,0:T(8,128)(2,1)}, bf16[64,30720]{1,0:T(8,128)(2,1)}, u32[]{:S(2)}, u32[]{:S(2)}) %collective-permute-start) | collective-permute-done | bytes 3932192 | tf_op jit(solution)/shard_map/ppermute | solution.py:21
  108.9 39.4 %filter_transform.7 = bf16[512,16,128]{2,1,0:T(8,128)(2,1)} custom-call(s32[16]{0:T(128)} %get-tuple-element.27.index_ref, bf16[64,196608]{1,0:T(8,128)(2,1)} %volt_ref.7, bf16[64,30720]{1,0:T(8,128)(2,1)} %collective-permute-done.halo_ref, f32[16,2048]{1,0:T(8,128)} %coef_ref.7, bf16[1024,2048]{1,0:T(8,128)(2,1)} %bitcast.12, f32[8,128]{1,0:T(8,128)} %slice.57.weight_ref), custom_call_target="tpu_custom_call" | custom-call | flops 17179869184 | bytes 12582912 | tf_op jit(solution)/shard_map/filter_transform/pallas_call | solution.py:158
  148.3 3.4 fusion.18
  151.7 3.7 all-to-all-start.3
  155.3 30.6 %filter_transform.6 = bf16[512,16,128]{2,1,0:T(8,128)(2,1)} custom-call(s32[16]{0:T(128)} %get-tuple-element.28.index_ref, bf16[64,196608]{1,0:T(8,128)(2,1)} %volt_ref.7, bf16[64,196608]{1,0:T(8,128)(2,1)} %volt_ref.7, f32[16,2048]{1,0:T(8,128)} %coef_ref.7, bf16[1024,2048]{1,0:T(8,128)(2,1)} %bitcast.13, f32[8,128]{1,0:T(8,128)} %slice.53.weight_ref), custom_call_target="tpu_custom_call" | custom-call | flops 17179869184 | bytes 12582912 | tf_op jit(solution)/shard_map/filter_transform/pallas_call | solution.py:158
  186.0 0.7 slice.50.weight_ref
  186.6 30.8 %filter_transform.5 = bf16[512,16,128]{2,1,0:T(8,128)(2,1)} custom-call(s32[16]{0:T(128)} %get-tuple-element.29.index_ref, bf16[64,196608]{1,0:T(8,128)(2,1)} %volt_ref.7, bf16[64,196608]{1,0:T(8,128)(2,1)} %volt_ref.7, f32[16,2048]{1,0:T(8,128)} %coef_ref.7, bf16[1024,2048]{1,0:T(8,128)(2,1)} %bitcast.14, f32[8,128]{1,0:T(8,128)} %slice.50.weight_ref), custom_call_target="tpu_custom_call" | custom-call | flops 17179869184 | bytes 12582912 | tf_op jit(solution)/shard_map/filter_transform/pallas_call | solution.py:158
  217.4 4.0 %pad_maximum_fusion.1 = bf16[16,2,32,16,128]{4,3,2,1,0:T(8,128)(2,1)} fusion(bf16[16,1,32,16,128]{4,3,2,1,0:T(8,128)(2,1)S(1)} %bitcast.17, bf16[16,1,32,16,128]{4,3,2,1,0:T(8,128)(2,1)} %bitcast.18), kind=kLoop, calls=%fused_computation.2 | loop fusion | flops 2097152 | bytes 8388608 | tf_op jit(solution)/shard_map/concatenate | solution.py:347
  221.4 107.4 %all_to_all.20.refs_2_ = bf16[16,2,32,16,128]{4,3,2,1,0:T(8,128)(2,1)} all-to-all(bf16[16,2,32,16,128]{4,3,2,1,0:T(8,128)(2,1)} %pad_maximum_fusion.1), channel_id=1, replica_groups=mesh['grp'=2,'inp'=4,'tblk'=2,'sub'=2] {'inp','tblk','sub'}, dimensions={0} | all-to-all | bytes 8388608 | tf_op jit(solution)/shard_map/all_to_all | solution.py:344
  328.8 5.3 %all-to-all-start.2 = ((bf16[16,1,16,16,128]{4,3,2,1,0:T(8,128)(2,1)}), bf16[16,1,16,16,128]{4,3,2,1,0:T(8,128)(2,1)S(1)}, u32[]{:S(2)}, u32[]{:S(2)}) async-start(bf16[16,1,16,16,128]{4,3,2,1,0:T(8,128)(2,1)} %get-tuple-element.16), calls=%async_computation.2 | async-start | bytes 2097152 | tf_op jit(solution)/shard_map/all_to_all | solution.py:344
  334.1 0.6 reduce_sum.36
  335.4 15.0 %correlate.2.refs_4_ = bf16[32,512,512]{2,1,0:T(8,128)(2,1)} custom-call(f32[1]{0:T(128)} %bitcast.refs_0_, bf16[16,1,32,16,128]{4,3,2,1,0:T(8,128)(2,1)} %copy-done, bf16[16,2,32,16,128]{4,3,2,1,0:T(8,128)(2,1)} %all_to_all.20.refs_2_, bf16[16,1,16,16,128]{4,3,2,1,0:T(8,128)(2,1)} %copy-done.3), custom_call_target="tpu_custom_call" | custom-call | flops 8589934592 | bytes 12582912 | tf_op jit(solution)/shard_map/correlate/pallas_call | solution.py:235
  350.4 6.6 %all-to-all-done.2.refs_3_ = bf16[16,1,16,16,128]{4,3,2,1,0:T(8,128)(2,1)S(1)} async-done(((bf16[16,1,16,16,128]{4,3,2,1,0:T(8,128)(2,1)}), bf16[16,1,16,16,128]{4,3,2,1,0:T(8,128)(2,1)S(1)}, u32[]{:S(2)}, u32[]{:S(2)}) %all-to-all-start.2) | async-done | bytes 1048608 | tf_op jit(solution)/shard_map/all_to_all | solution.py:344
  357.0 1.0 copy-done.1
  358.0 15.0 %correlate.3 = bf16[32,512,512]{2,1,0:T(8,128)(2,1)} custom-call(f32[1]{0:T(128)} %bitcast.refs_0_, bf16[16,1,32,16,128]{4,3,2,1,0:T(8,128)(2,1)} %copy-done, bf16[16,2,32,16,128]{4,3,2,1,0:T(8,128)(2,1)} %all_to_all.20.refs_2_, bf16[16,1,16,16,128]{4,3,2,1,0:T(8,128)(2,1)} %copy-done.1, ...), custom_call_target="tpu_custom_call", output_to_operand_aliasing={{}: (4, {})} | custom-call | flops 8589934592 | bytes 12582912 | tf_op jit(solution)/shard_map/correlate/pallas_call | solution.py:235
  (19 shorter events, 0.1 us)
Async XLA Ops:
  0.0 11.1 %copy-start.5 = (s32[192]{0:T(256)S(1)}, s32[192]{0:T(256)}, u32[]{:S(2)}) copy-start(s32[192]{0:T(256)} %param.8) | copy-start | bytes 2308
  0.0 12.7 %copy-start.6 = (s32[64,96]{1,0:T(8,128)S(1)}, s32[64,96]{1,0:T(8,128)}, u32[]{:S(2)}) copy-start(s32[64,96]{1,0:T(8,128)} %param.7) | copy-start | bytes 73732
  0.0 12.9 %copy-start.4 = (s32[512]{0:T(512)S(1)}, s32[512]{0:T(512)}, u32[]{:S(2)}) copy-start(s32[512]{0:T(512)} %param.9) | copy-start | bytes 6148
  4.3 104.6 %collective-permute-start = (bf16[64,30720]{1,0:T(8,128)(2,1)}, bf16[64,30720]{1,0:T(8,128)(2,1)}, u32[]{:S(2)}, u32[]{:S(2)}) collective-permute-start(bf16[64,30720]{1,0:T(8,128)(2,1)} %slice.55), channel_id=1, source_target_pairs={{0,2},{1,3},{4,6},{5,7},{8,10},{9,11},{12,14},{13,15},{16,18},{17,... | collective-permute-start | bytes 11796488 | tf_op jit(solution)/shard_map/ppermute | solution.py:21
  69.1 82.6 %all-to-all-start = ((bf16[16,1,32,16,128]{4,3,2,1,0:T(8,128)(2,1)}), bf16[16,1,32,16,128]{4,3,2,1,0:T(8,128)(2,1)S(1)}, u32[]{:S(2)}, u32[]{:S(2)}) async-start(bf16[16,1,32,16,128]{4,3,2,1,0:T(8,128)(2,1)} %bitcast.15), calls=%async_computation | async-start | bytes 4194304 | tf_op jit(solution)/shard_map/all_to_all | solution.py:344
  151.7 34.3 %copy-start = (bf16[16,1,32,16,128]{4,3,2,1,0:T(8,128)(2,1)}, bf16[16,1,32,16,128]{4,3,2,1,0:T(8,128)(2,1)S(1)}, u32[]{:S(2)}) copy-start(bf16[16,1,32,16,128]{4,3,2,1,0:T(8,128)(2,1)S(1)} %all-to-all-done.refs_1_) | copy-start | bytes 6291460
  151.7 69.7 %all-to-all-start.3 = ((bf16[16,1,16,16,128]{4,3,2,1,0:T(8,128)(2,1)}), bf16[16,1,16,16,128]{4,3,2,1,0:T(8,128)(2,1)S(1)}, u32[]{:S(2)}, u32[]{:S(2)}) async-start(bf16[16,1,16,16,128]{4,3,2,1,0:T(8,128)(2,1)} %get-tuple-element.15), calls=%async_computation.3 | async-start | bytes 2097152 | tf_op jit(solution)/shard_map/all_to_all | solution.py:344
  186.6 30.8 %copy-start.2 = (bf16[512,16,128]{2,1,0:T(8,128)(2,1)S(1)}, bf16[512,16,128]{2,1,0:T(8,128)(2,1)}, u32[]{:S(2)}) copy-start(bf16[512,16,128]{2,1,0:T(8,128)(2,1)} %filter_transform.6) | copy-start | bytes 6291460
  221.4 107.4 %copy-start.3 = (bf16[16,1,16,16,128]{4,3,2,1,0:T(8,128)(2,1)}, bf16[16,1,16,16,128]{4,3,2,1,0:T(8,128)(2,1)S(1)}, u32[]{:S(2)}) copy-start(bf16[16,1,16,16,128]{4,3,2,1,0:T(8,128)(2,1)S(1)} %all-to-all-done.3.refs_3_) | copy-start | bytes 3145732
  328.8 28.3 %all-to-all-start.2 = ((bf16[16,1,16,16,128]{4,3,2,1,0:T(8,128)(2,1)}), bf16[16,1,16,16,128]{4,3,2,1,0:T(8,128)(2,1)S(1)}, u32[]{:S(2)}, u32[]{:S(2)}) async-start(bf16[16,1,16,16,128]{4,3,2,1,0:T(8,128)(2,1)} %get-tuple-element.16), calls=%async_computation.2 | async-start | bytes 2097152 | tf_op jit(solution)/shard_map/all_to_all | solution.py:344
  357.0 1.0 copy-start.1

commit v2 on v0

--- a/solution.py
+++ b/solution.py
@@ -1,9 +1,19 @@
+import functools
 import math
 
 import jax
 import jax.numpy as jnp
 from jax import lax
+from jax.experimental import pallas as pl
+from jax.experimental.pallas import tpu as pltpu
 from jax.sharding import PartitionSpec as P
+
+MAX_KEPT = 64
+STEP = 16
+LANES = 128
+COLS = 256
+AHEAD = 8
+VMEM_BYTES = 56 * 1024 * 1024
 
 
 def passed_along(value, axis, steps):
@@ -12,7 +22,274 @@
     return lax.ppermute(value, axis, [(source, source + steps) for source in range(initial, last)])
 
 
-def make_table(channels, frame_len):
+def fill_table(chan_ref, table_ref, frame_len):
+    slots = chan_ref.shape[0]
+    scale = 2.0 * math.pi / frame_len
+    norm_scale = 1.0 / math.sqrt(frame_len)
+
+    def block(step, carry):
+        rows = pl.ds(pl.multiple_of(step * 64, 64), 64)
+        lane = lax.broadcasted_iota(jnp.int32, (64, LANES), 1)
+        channels = chan_ref[rows, :]
+        fine = lax.rem(channels * lane, frame_len).astype(jnp.float32) * scale
+        coarse = lax.rem(channels * lane * LANES, frame_len).astype(jnp.float32) * scale
+        fine_cos, fine_sin = jnp.cos(fine), jnp.sin(fine)
+        coarse_cos, coarse_sin = jnp.cos(coarse) * norm_scale, jnp.sin(coarse) * norm_scale
+        for part in range(frame_len // LANES):
+            span = pl.ds(part * LANES, LANES)
+            cosine, sine = coarse_cos[:, part : part + 1], coarse_sin[:, part : part + 1]
+            below = pl.ds(pl.multiple_of(slots + step * 64, 64), 64)
+            table_ref[rows, span] = (cosine * fine_cos - sine * fine_sin).astype(table_ref.dtype)
+            table_ref[below, span] = -(sine * fine_cos + cosine * fine_sin).astype(table_ref.dtype)
+        return carry
+
+    lax.fori_loop(0, slots // 64, block, 0)
+
+
+def transform_kernel(row_first, rows, with_halo, starts, *refs):
+    place_ref, good_ref, flag_ref, volt_ref, coef_ref, halo_ref, table_in, _, *refs = refs
+    if starts:
+        out_ref, table_ref, last_ref, *refs = refs
+    else:
+        out_ref, *refs = refs
+        table_ref = table_in
+    index_ref, raw, wide, hot, weight, filt, turn, sems, last_sem = refs
+    taps, frame_len = coef_ref.shape
+    ins, block_len = flag_ref.shape
+    slots = table_ref.shape[0] // 2
+    ring, ahead = wide.shape[0], raw.shape[0]
+    pairs = rows * ins // LANES
+
+    def note(s, carry):
+        seen, latest = carry
+        keep = good_ref[place_ref[0] * block_len + s] > 0
+        mine = keep & (seen >= row_first) & (seen < row_first + rows)
+
+        @pl.when(mine)
+        def _():
+            index_ref[seen - row_first] = s
+
+        return seen + keep.astype(jnp.int32), jnp.where(mine, s, latest)
+
+    seen, latest = lax.fori_loop(0, block_len, note, (jnp.int32(0), jnp.int32(block_len - 1)))
+    used = jnp.clip(seen - row_first, 0, rows)
+
+    def rest(r, carry):
+        index_ref[r] = latest
+        return carry
+
+    lax.fori_loop(used, rows, rest, 0)
+    first = index_ref[0]
+    end = index_ref[rows - 1] + taps
+
+    def on_copy(extended, act):
+        slot = lax.rem(extended, ahead)
+
+        def one(ref, frame):
+            begin = pl.multiple_of(frame * frame_len, frame_len)
+            act(pltpu.make_async_copy(ref.at[:, pl.ds(begin, frame_len)], raw.at[slot], sems.at[slot]))
+
+        if with_halo:
+
+            @pl.when(extended < taps - 1)
+            def _():
+                one(halo_ref, extended)
+
+        @pl.when(extended >= taps - 1)
+        def _():
+            one(volt_ref, extended - (taps - 1))
+
+    def fetch(extended):
+        @pl.when(extended < end)
+        def _():
+            on_copy(extended, lambda c: c.start())
+
+    for k in range(ahead):
+        fetch(first + k)
+    if starts:
+        pass_on = pltpu.make_async_copy(
+            volt_ref.at[:, pl.ds((block_len - taps + 1) * frame_len, (taps - 1) * frame_len)], last_ref, last_sem
+        )
+        pass_on.start()
+        fill_table(table_in, table_ref, frame_len)
+
+    spectrum = lax.broadcasted_iota(jnp.int32, (1, block_len), 1)
+    for r in range(rows):
+        chosen = (spectrum == index_ref[r]) & (jnp.int32(r) < used)
+        hot[pl.ds((r % 2) * (rows // 2) + r // 2, 1), :] = chosen.astype(jnp.float32)
+    flags = flag_ref[...].astype(jnp.float32)
+    weights = lax.dot_general(hot[...], flags, (((1,), (1,)), ((), ())), preferred_element_type=jnp.float32)
+    weight[...] = jnp.concatenate([weights[: rows // 2], weights[rows // 2 :]], axis=1)
+
+    def take(extended, carry):
+        on_copy(extended, lambda c: c.wait())
+        to, came = lax.rem(extended, ring), lax.rem(extended, ahead)
+        for col in range(frame_len // LANES):
+            wide[to, col] = raw[came, :, col * LANES : (col + 1) * LANES].astype(jnp.float32)
+        fetch(extended + ahead)
+        return carry
+
+    def row(r, have):
+        base = index_ref[r]
+        lax.fori_loop(have, base + taps, take, 0)
+        places = [lax.rem(base + k, ring) for k in range(taps)]
+        at = pl.ds(pl.multiple_of(r * ins, ins), ins)
+        for col in range(frame_len // LANES):
+            here = pl.ds(col * LANES, LANES)
+            total = None
+            for k in range(taps):
+                term = wide[places[k], col] * coef_ref[pl.ds(k, 1), here]
+                total = term if total is None else total + term
+            filt[at, here] = total.astype(jnp.bfloat16)
+        return jnp.maximum(have, base + taps)
+
+    lax.fori_loop(0, rows, row, first)
+
+    per_dot = COLS // LANES
+
+    def multiply(m, carry):
+        here = pl.ds(pl.multiple_of(m * COLS, COLS), COLS)
+        for n in range(pairs // per_dot):
+            spec = lax.dot_general(
+                table_ref[here, :],
+                filt[pl.ds(n * COLS, COLS), :],
+                (((1,), (1,)), ((), ())),
+                preferred_element_type=jnp.float32,
+            )
+            for h in range(per_dot):
+                b = n * per_dot + h
+                turn[pl.ds(pl.multiple_of(b * 2 * slots + m * COLS, COLS), COLS), :] = (
+                    spec[:, h * LANES : (h + 1) * LANES] * weight[pl.ds(b, 1), :]
+                )
+        return carry
+
+    lax.fori_loop(0, 2 * slots // COLS, multiply, 0)
+
+    def corner(j, carry):
+        for u in range(8):
+            slot = j * 8 + u
+            real = turn[pl.ds(slot, pairs, stride=2 * slots), :]
+            imag = turn[pl.ds(slots + slot, pairs, stride=2 * slots), :]
+            out_ref[slot] = jnp.concatenate([real, imag], axis=0).astype(jnp.bfloat16)
+        return carry
+
+    lax.fori_loop(0, slots // 8, corner, 0)
+    if starts:
+        pass_on.wait()
+
+
+def transform(place, spec_good, input_flags, voltages, coefs, halo, table, after, row_first, rows):
+    ins, block_len = input_flags.shape
+    taps, frame_len = coefs.shape
+    starts = table.ndim == 2 and table.shape[1] == 1
+    slots = table.shape[0] if starts else table.shape[0] // 2
+    pairs = rows * ins // LANES
+    flops = 2 * rows * ins * frame_len * 2 * slots
+    smem = pl.BlockSpec(memory_space=pltpu.SMEM)
+    vmem = pl.BlockSpec(memory_space=pltpu.VMEM)
+    hbm = pl.BlockSpec(memory_space=pl.ANY)
+    out_shape = [jax.ShapeDtypeStruct((slots, 2 * pairs, LANES), jnp.bfloat16)]
+    out_specs = [vmem]
+    if starts:
+        out_shape.append(jax.ShapeDtypeStruct((2 * slots, frame_len), jnp.bfloat16))
+        out_shape.append(jax.ShapeDtypeStruct((ins, (taps - 1) * frame_len), jnp.bfloat16))
+        out_specs += [vmem, hbm]
+    return pl.pallas_call(
+        functools.partial(transform_kernel, row_first, rows, halo is not None, starts),
+        out_shape=out_shape,
+        in_specs=[smem, smem, vmem, hbm, vmem, hbm, vmem, hbm],
+        out_specs=out_specs,
+        scratch_shapes=[
+            pltpu.SMEM((rows,), jnp.int32),
+            pltpu.VMEM((AHEAD, ins, frame_len), jnp.bfloat16),
+            pltpu.VMEM((taps, frame_len // LANES, ins, LANES), jnp.float32),
+            pltpu.VMEM((rows, block_len), jnp.float32),
+            pltpu.VMEM((pairs, LANES), jnp.float32),
+            pltpu.VMEM((rows * ins, frame_len), jnp.bfloat16),
+            pltpu.VMEM((pairs * 2 * slots, LANES), jnp.float32),
+            pltpu.SemaphoreType.DMA((AHEAD,)),
+            pltpu.SemaphoreType.DMA,
+        ],
+        compiler_params=pltpu.CompilerParams(vmem_limit_bytes=VMEM_BYTES),
+        cost_estimate=pl.CostEstimate(flops=4 * flops, bytes_accessed=12 * 2**20, transcendentals=0),
+        name="filter_transform",
+    )(place, spec_good, input_flags, voltages, coefs, voltages if halo is None else halo, table, voltages if after is None else after)
+
+
+def correlate_kernel(blocks, chips, cores, pieces, *refs):
+    scale_ref, refs = refs[0], refs[1:]
+    part_refs = refs[:pieces]
+    out_ref, straight, turned = refs[-3:]
+    ins = LANES // cores
+    total = straight.shape[1]
+    for chip in range(chips):
+        lanes = pl.ds(chip * LANES, LANES)
+        place = 0
+        for block in range(blocks):
+            sources = [(chip * blocks + block) * cores + core for core in range(cores)]
+            for part in part_refs:
+                depth = part.shape[2]
+                half_depth = depth // 2
+                one, two = (part[source, 0].astype(jnp.float32) for source in sources)
+                low = lax.broadcasted_iota(jnp.int32, (depth, LANES), 1) < ins
+                first = jnp.where(low, one, pltpu.roll(two, ins, 1))
+                second = jnp.where(low, pltpu.roll(one, ins, 1), two)
+                for both in (first, second):
+                    rows = pl.ds(place, depth)
+                    straight[rows, lanes] = both.astype(jnp.bfloat16)
+                    turned[rows, lanes] = jnp.concatenate([-both[half_depth:], both[:half_depth]], axis=0).astype(jnp.bfloat16)
+                    place += depth
+    left = straight[...].T
+    scale = scale_ref[0]
+    half = total // 2
+
+    def product(a, ref, b):
+        return jnp.dot(left[a * half : (a + 1) * half], ref[:, b * half : (b + 1) * half], preferred_element_type=jnp.float32) * scale
+
+    upper = lax.broadcasted_iota(jnp.int32, (half, half), 1) >= lax.broadcasted_iota(jnp.int32, (half, half), 0)
+    for a in range(2):
+        here = pl.ds(a * half, half)
+        both = jnp.where(upper, product(a, straight, a), product(a, turned, a))
+        out_ref[0, here, here] = both.astype(out_ref.dtype)
+    out_ref[0, :half, half:] = product(0, straight, 1).astype(out_ref.dtype)
+    out_ref[0, half:, :half] = product(1, turned, 0).astype(out_ref.dtype)
+
+
+def correlate(scale, parts, into, first, own, blocks, chips, cores):
+    count = min(part.shape[1] - begin for part, begin in parts)
+    sources = blocks * chips * cores
+    total = chips * LANES
+    depth = blocks * cores * sum(part.shape[2] for part, _ in parts)
+
+    def spec(part, begin):
+        return pl.BlockSpec((sources, 1) + part.shape[2:], lambda c: (0, c + begin, 0, 0))
+
+    arrays = [part for part, _ in parts]
+    in_specs = [pl.BlockSpec(memory_space=pltpu.SMEM)] + [spec(*pair) for pair in parts]
+    operands = [scale] + arrays
+    aliases = {}
+    kernel = functools.partial(correlate_kernel, blocks, chips, cores, len(parts))
+    if into is not None:
+        aliases = {len(operands): 0}
+        operands.append(into)
+        in_specs.append(pl.BlockSpec(memory_space=pl.ANY))
+    return pl.pallas_call(
+        kernel,
+        grid=(count,),
+        out_shape=jax.ShapeDtypeStruct((own, total, total), jnp.bfloat16),
+        in_specs=in_specs,
+        out_specs=pl.BlockSpec((1, total, total), lambda c: (c + first, 0, 0)),
+        scratch_shapes=[pltpu.VMEM((depth, total), jnp.bfloat16)] * 2,
+        input_output_aliases=aliases,
+        compiler_params=pltpu.CompilerParams(vmem_limit_bytes=VMEM_BYTES),
+        cost_estimate=pl.CostEstimate(
+            flops=count * 8 * total * total * depth, bytes_accessed=count * 3 * total * total, transcendentals=0
+        ),
+        name="correlate",
+    )(*operands)
+
+
+def make_plain_table(channels, frame_len):
     samples = jnp.arange(frame_len, dtype=jnp.int32)
     phase_index = samples[:, None] * channels[None, :] % frame_len
     angles = phase_index.astype(jnp.float32) * (2.0 * math.pi / frame_len)
@@ -38,7 +315,7 @@
     return lax.optimization_barrier(values.astype(jnp.bfloat16)).astype(jnp.float32)
 
 
-def local(voltages, pfb_coeffs, input_flags, spec_good, chan_map):
+def local_plain(voltages, pfb_coeffs, input_flags, spec_good, chan_map):
     tap_count, frame_len = pfb_coeffs.shape
     local_inputs, block_len = input_flags.shape
     frames = voltages.reshape(local_inputs, block_len, frame_len)
@@ -60,7 +337,7 @@
     live_total = jnp.sum(spec_good).astype(jnp.float32)
     slot_order = jnp.arange(chan_total).reshape(inp_count, tblk_count, sub_count, per_owner)
     slot_order = slot_order.transpose(0, 2, 1, 3).reshape(chan_total)
-    dft_table = make_table(chan_map[slot_order], frame_len)
+    dft_table = make_plain_table(chan_map[slot_order], frame_len)
     spectra = jnp.einsum("isn,nqj->jiqs", filtered, dft_table, preferred_element_type=jnp.float32)
     spectra = spectra.astype(jnp.bfloat16).reshape(chan_total, local_inputs, -1)
     turned = lax.all_to_all(spectra, ("inp", "sub"), split_axis=0, concat_axis=1, tiled=True)
@@ -71,6 +348,41 @@
         tiled=True,
     ).astype(jnp.float32)
     return (summed_vis / live_total).astype(jnp.bfloat16)
+
+
+def local(voltages, pfb_coeffs, input_flags, spec_good, chan_map):
+    taps, frame_len = pfb_coeffs.shape
+    ins, block_len = input_flags.shape
+    chips, blocks, cores = (lax.axis_size(axis) for axis in ("inp", "tblk", "sub"))
+    owners = chips * blocks * cores
+    slots = chan_map.shape[0]
+    own = slots // owners
+    if ins * cores != LANES or own % 4 or ins % 16 or slots % 64:
+        return local_plain(voltages, pfb_coeffs, input_flags, spec_good, chan_map)
+    place = lax.axis_index("tblk").astype(jnp.int32).reshape(1)
+    scale = (1.0 / jnp.sum(spec_good).astype(jnp.float32)).reshape(1)
+
+    def chunk(row_first, rows, halo, table, after):
+        done, *more = transform(
+            place, spec_good, input_flags, voltages, pfb_coeffs, halo, table, after, row_first, rows
+        )
+        return [done.reshape(owners, own, *done.shape[1:])] + more
+
+    def turn(piece):
+        return lax.all_to_all(piece, ("inp", "tblk", "sub"), split_axis=0, concat_axis=0, tiled=True)
+
+    early, table, last_frames = chunk(STEP, STEP, None, chan_map.reshape(slots, 1), None)
+    turned = [(turn(early), 0)]
+    halo = passed_along(last_frames, "tblk", 1)
+    (middle,) = chunk(2 * STEP, 2 * STEP, None, table, early)
+    turned.append((turn(middle), 0))
+    (late,) = chunk(0, STEP, halo, table, middle)
+    out = None
+    for begin, end in ((0, own * 3 // 4), (own * 3 // 4, own)):
+        tail = turn(late[:, begin:end])
+        parts = [(part, begin) for part, _ in turned] + [(tail, 0)]
+        out = correlate(scale, parts, out, begin, own, blocks, chips, cores)
+    return out
 
 
 def solution(mesh):

time: 1400 us -> 443 us (0.32)
  waiting for transfers between devices: 793 us -> 126 us
  other arithmetic: 362 us -> 0.63 us
  Pallas kernels: 0 us -> 226 us
  local copies, waits for them, and re-layouts: 156 us -> 7.1 us
  matrix products: 62.3 us -> 0 us
  blocking collectives: 0 us -> 44.4 us
  starting transfers between devices: 12.5 us -> 36.6 us
    reduce_scatter x1 -> x0, waiting for transfers between devices: 368 us -> none  [local(): lax.psum_scatter(rounded(lax.map(correlate_one, turned)).astype(jnp.bfloa...]
    all_to_all x1 -> x3, waiting for transfers between devices: 364 us -> 74.5 us  [turn(): lax.all_to_all(piece, ('inp', 'tblk', 'sub'), split_axis=0, concat_axis=0...]
    dot_general x1 -> x0, other arithmetic: 266 us -> none  [local(): jnp.einsum('isn,nqj->jiqs', filtered, dft_table, preferred_element_type=j...]
    pallas_call x0 -> x5, Pallas kernels: none -> 226 us  [the longest x3 196 us: transform(): pl.pallas_call(functools.partial(transform_kernel, row_first, rows, halo...]
    dot_general x65 -> x0, matrix products: 62.3 us -> none  [the longest x1 31.4 us: local(): jnp.einsum('isn,nqj->jiqs', filtered, dft_table, preferred_element_type=j...]
    squeeze x64 -> x0, local copies, waits for them, and re-layouts: 61.9 us -> none  [local(): lax.map(correlate_one, turned)]
    dynamic_update_slice x64 -> x0, other arithmetic: 56.2 us -> none  [local(): lax.map(correlate_one, turned)]
    all_to_all x0 -> x1, blocking collectives: none -> 44.4 us  [turn(): lax.all_to_all(piece, ('inp', 'tblk', 'sub'), split_axis=0, concat_axis=0...]
  transfers between devices with their start and end apart: 3 -> 4, of which waited for: 3 -> 2; matrix products, arithmetic and copies ran while one was open for 2% -> 1% of each run, Pallas kernels for 0% -> 21%
where the time goes in v2:
time: 443 us; the launch traced here: 442 us
  Pallas kernels  226 us (51%)
  waiting for transfers between devices  126 us (28%)
  blocking collectives  44.4 us (10%)
  starting transfers between devices  36.6 us (8%)
  local copies, waits for them, and re-layouts  7.1 us (2%)
    pallas_call x3, Pallas kernels, transform(): pl.pallas_call(functools.partial(transform_kernel, row_first, rows, halo...  196 us
    all_to_all x3, waiting for transfers between devices, turn(): lax.all_to_all(piece, ('inp', 'tblk', 'sub'), split_axis=0, concat_axis=0...  74.5 us
    ppermute x1, waiting for transfers between devices, passed_along(): lax.ppermute(value, axis, [(source, source + steps) for source in range(i...  51.8 us
    all_to_all x1, blocking collectives, turn(): lax.all_to_all(piece, ('inp', 'tblk', 'sub'), split_axis=0, concat_axis=0...  44.4 us
    pallas_call x2, Pallas kernels, correlate(): pl.pallas_call(kernel, grid=(count,), out_shape=jax.ShapeDtypeStruct((own...  29.9 us
    all_to_all x3, starting transfers between devices, turn(): lax.all_to_all(piece, ('inp', 'tblk', 'sub'), split_axis=0, concat_axis=0...  29.8 us
  transfers between devices with their start and end apart: 4, of which 2 were waited for; matrix products, arithmetic and copies ran while one was open for 1% of the time, Pallas kernels for 21%

profile of v2, /device:TPU:0, one launch (start us, length us, event | category | flops | bytes accessed | tf_op | source)
XLA Modules:
  0.0 442.0 jit_solution(4083696193001933644)
XLA Ops:
  0.0 1.5 copy.7.refs_6_
  1.5 125.9 %filter_transform.3 = (bf16[512,16,128]{2,1,0:T(8,128)(2,1)}, bf16[1024,2048]{1,0:T(8,128)(2,1)}, bf16[64,30720]{1,0:T(8,128)(2,1)}) custom-call(s32[1]{0:T(128)} %bitcast.1.refs_0_, s32[192]{0:T(256)} %refs_1_.5, s32[64,96]{1,0:T(8,128)} %refs_2_.5, bf16[64,196608]{1,0:T(8,128)(2,1)} %refs_3_.5, f32[16,2048]{1,0:T(8,128)} %refs_4_.5, ...), custom_call_target="tpu_custom_call" | custom-call | flops 17179869184 | bytes 12582912 | tf_op jit(solution)/shard_map/filter_transform/pallas_call | solution.py:197
  127.4 6.8 %collective-permute-start = (bf16[64,30720]{1,0:T(8,128)(2,1)}, bf16[64,30720]{1,0:T(8,128)(2,1)}, u32[]{:S(2)}, u32[]{:S(2)}) collective-permute-start(bf16[64,30720]{1,0:T(8,128)(2,1)} %get-tuple-element.10), channel_id=1, source_target_pairs={{0,2},{1,3},{4,6},{5,7},{8,10},{9,11},{12,14},{13,15},{16,18},{17,... | collective-permute-start | bytes 11796488 | tf_op jit(solution)/shard_map/ppermute | solution.py:22
  134.2 5.0 %all-to-all-start = ((bf16[16,32,16,128]{3,2,1,0:T(8,128)(2,1)}), bf16[16,32,16,128]{3,2,1,0:T(8,128)(2,1)S(1)}, u32[]{:S(2)}, u32[]{:S(2)}) async-start(bf16[16,32,16,128]{3,2,1,0:T(8,128)(2,1)} %bitcast.10), calls=%async_computation | async-start | bytes 4194304 | tf_op jit(solution)/shard_map/all_to_all | solution.py:372
  139.2 43.8 %filter_transform.4 = bf16[512,32,128]{2,1,0:T(8,128)(2,1)} custom-call(s32[1]{0:T(128)} %bitcast.1.refs_0_, s32[192]{0:T(256)} %refs_1_.5, s32[64,96]{1,0:T(8,128)} %refs_2_.5, bf16[64,196608]{1,0:T(8,128)(2,1)} %refs_3_.5, f32[16,2048]{1,0:T(8,128)} %refs_4_.5, bf16[64,196608]{1,0:T(8,128)(2,1)} %refs_3_.5, bf16[1024,2048]{1,0:T(8,128)(2,1)} %get-tuple-element.9.refs_6_, ...), custom_call_target="tpu_custom_call" | custom-call | flops 34359738368 | bytes 12582912 | tf_op jit(solution)/shard_map/filter_transform/pallas_call | solution.py:197
  183.0 51.8 %collective-permute-done.refs_5_ = bf16[64,30720]{1,0:T(8,128)(2,1)} collective-permute-done((bf16[64,30720]{1,0:T(8,128)(2,1)}, bf16[64,30720]{1,0:T(8,128)(2,1)}, u32[]{:S(2)}, u32[]{:S(2)}) %collective-permute-start) | collective-permute-done | bytes 3932192 | tf_op jit(solution)/shard_map/ppermute | solution.py:22
  234.8 26.7 %filter_transform.5 = bf16[512,16,128]{2,1,0:T(8,128)(2,1)} custom-call(s32[1]{0:T(128)} %bitcast.1.refs_0_, s32[192]{0:T(256)} %refs_1_.5, s32[64,96]{1,0:T(8,128)} %refs_2_.5, bf16[64,196608]{1,0:T(8,128)(2,1)} %refs_3_.5, f32[16,2048]{1,0:T(8,128)} %refs_4_.5, bf16[64,30720]{1,0:T(8,128)(2,1)} %collective-permute-done.refs_5_, ...), custom_call_target="tpu_custom_call" | custom-call | flops 17179869184 | bytes 12582912 | tf_op jit(solution)/shard_map/filter_transform/pallas_call | solution.py:197
  261.5 2.9 slice.9
  264.3 0.0 all-to-all-done.refs_1_
  264.4 0.0 copy-start
  264.4 44.4 %all_to_all.20.refs_3_ = bf16[16,24,16,128]{3,2,1,0:T(8,128)(2,1)} all-to-all(bf16[16,24,16,128]{3,2,1,0:T(8,128)(2,1)} %slice.9), channel_id=1, replica_groups=mesh['grp'=2,'inp'=4,'tblk'=2,'sub'=2] {'inp','tblk','sub'}, dimensions={0} | all-to-all | bytes 3145728 | tf_op jit(solution)/shard_map/all_to_all | solution.py:372
  308.8 0.0 copy-start.2
  308.8 0.0 copy-done
  308.8 5.2 %all-to-all-start.1 = ((bf16[16,32,32,128]{3,2,1,0:T(8,128)(2,1)}), bf16[16,32,32,128]{3,2,1,0:T(8,128)(2,1)}, u32[]{:S(2)}, u32[]{:S(2)}) async-start(bf16[16,32,32,128]{3,2,1,0:T(8,128)(2,1)} %bitcast.7), calls=%async_computation.1 | async-start | bytes 8388608 | tf_op jit(solution)/shard_map/all_to_all | solution.py:372
  314.0 0.0 copy-done.2
  314.0 0.6 reduce_sum.9
  315.3 1.9 slice.8
  317.2 74.5 %all-to-all-done.1.refs_2_ = bf16[16,32,32,128]{3,2,1,0:T(8,128)(2,1)} async-done(((bf16[16,32,32,128]{3,2,1,0:T(8,128)(2,1)}), bf16[16,32,32,128]{3,2,1,0:T(8,128)(2,1)}, u32[]{:S(2)}, u32[]{:S(2)}) %all-to-all-start.1) | async-done | bytes 4194336 | tf_op jit(solution)/shard_map/all_to_all | solution.py:372
  391.7 19.6 %all-to-all-start.2 = ((bf16[16,8,16,128]{3,2,1,0:T(8,128)(2,1)}), bf16[16,8,16,128]{3,2,1,0:T(8,128)(2,1)S(1)}, u32[]{:S(2)}, u32[]{:S(2)}) async-start(bf16[16,8,16,128]{3,2,1,0:T(8,128)(2,1)} %slice.8), calls=%async_computation.2 | async-start | bytes 1048576 | tf_op jit(solution)/shard_map/all_to_all | solution.py:372
  411.3 21.8 %correlate.2.refs_4_ = bf16[32,512,512]{2,1,0:T(8,128)(2,1)} custom-call(f32[1]{0:T(128)} %bitcast.refs_0_, bf16[16,32,16,128]{3,2,1,0:T(8,128)(2,1)} %copy-done, bf16[16,32,32,128]{3,2,1,0:T(8,128)(2,1)} %all-to-all-done.1.refs_2_, bf16[16,24,16,128]{3,2,1,0:T(8,128)(2,1)} %all_to_all.20.refs_3_), custom_call_target="tpu_custom_call" | custom-call | flops 12884901888 | bytes 18874368 | tf_op jit(solution)/shard_map/correlate/pallas_call | solution.py:276
  433.2 0.0 all-to-all-done.2.refs_3_
  433.2 0.0 copy-start.1
  433.2 0.8 copy-done.1
  434.0 8.1 %correlate.3 = bf16[32,512,512]{2,1,0:T(8,128)(2,1)} custom-call(f32[1]{0:T(128)} %bitcast.refs_0_, bf16[16,32,16,128]{3,2,1,0:T(8,128)(2,1)} %copy-done, bf16[16,32,32,128]{3,2,1,0:T(8,128)(2,1)} %all-to-all-done.1.refs_2_, bf16[16,8,16,128]{3,2,1,0:T(8,128)(2,1)} %copy-done.1, bf16[32,512,512]{2,1,0:T(8,128)(2,1)} %correlate.2.refs_4_), custom_call_target="tpu_custom_call", output_to_operand_aliasing={{}: (4, {})} | custom-call | flops 4294967296 | bytes 6291456 | tf_op jit(solution)/shard_map/correlate/pallas_call | solution.py:276
Async XLA Ops:
  127.4 107.4 %collective-permute-start = (bf16[64,30720]{1,0:T(8,128)(2,1)}, bf16[64,30720]{1,0:T(8,128)(2,1)}, u32[]{:S(2)}, u32[]{:S(2)}) collective-permute-start(bf16[64,30720]{1,0:T(8,128)(2,1)} %get-tuple-element.10), channel_id=1, source_target_pairs={{0,2},{1,3},{4,6},{5,7},{8,10},{9,11},{12,14},{13,15},{16,18},{17,... | collective-permute-start | bytes 11796488 | tf_op jit(solution)/shard_map/ppermute | solution.py:22
  134.2 130.2 %all-to-all-start = ((bf16[16,32,16,128]{3,2,1,0:T(8,128)(2,1)}), bf16[16,32,16,128]{3,2,1,0:T(8,128)(2,1)S(1)}, u32[]{:S(2)}, u32[]{:S(2)}) async-start(bf16[16,32,16,128]{3,2,1,0:T(8,128)(2,1)} %bitcast.10), calls=%async_computation | async-start | bytes 4194304 | tf_op jit(solution)/shard_map/all_to_all | solution.py:372
  264.4 44.4 %copy-start = (bf16[16,32,16,128]{3,2,1,0:T(8,128)(2,1)}, bf16[16,32,16,128]{3,2,1,0:T(8,128)(2,1)S(1)}, u32[]{:S(2)}) copy-start(bf16[16,32,16,128]{3,2,1,0:T(8,128)(2,1)S(1)} %all-to-all-done.refs_1_) | copy-start | bytes 6291460
  308.8 5.2 %copy-start.2 = (s32[192]{0:T(256)S(1)}, s32[192]{0:T(256)}, u32[]{:S(2)}) copy-start(s32[192]{0:T(256)} %refs_1_.5) | copy-start | bytes 2308
  308.8 82.9 %all-to-all-start.1 = ((bf16[16,32,32,128]{3,2,1,0:T(8,128)(2,1)}), bf16[16,32,32,128]{3,2,1,0:T(8,128)(2,1)}, u32[]{:S(2)}, u32[]{:S(2)}) async-start(bf16[16,32,32,128]{3,2,1,0:T(8,128)(2,1)} %bitcast.7), calls=%async_computation.1 | async-start | bytes 8388608 | tf_op jit(solution)/shard_map/all_to_all | solution.py:372
  391.7 41.5 %all-to-all-start.2 = ((bf16[16,8,16,128]{3,2,1,0:T(8,128)(2,1)}), bf16[16,8,16,128]{3,2,1,0:T(8,128)(2,1)S(1)}, u32[]{:S(2)}, u32[]{:S(2)}) async-start(bf16[16,8,16,128]{3,2,1,0:T(8,128)(2,1)} %slice.8), calls=%async_computation.2 | async-start | bytes 1048576 | tf_op jit(solution)/shard_map/all_to_all | solution.py:372
  433.2 0.8 copy-start.1

commit v3 on v2

v3 whole, which is shorter than its diff:
```python
import functools
import math

import jax
import jax.numpy as jnp
from jax import lax
from jax.experimental import pallas as pl
from jax.experimental.pallas import tpu as pltpu
from jax.sharding import PartitionSpec as P

MAX_KEPT = 64
STEP = 16
LANES = 128
COLS = 256
SLOTS = 4
BLOCKS = 2
AHEAD = 8
VMEM_BYTES = 56 * 1024 * 1024


def passed_along(value, axis, steps):
    count = lax.axis_size(axis)
    initial, last = (max(0, -steps), min(count, count - steps))
    return lax.ppermute(value, axis, [(source, source + steps) for source in range(initial, last)])


def turn_of(places, frame_len):
    quarter = frame_len // 4
    turns = (places + quarter // 2) // quarter
    angle = (places - turns * quarter).astype(jnp.float32) * (2.0 * math.pi / frame_len)
    square = angle * angle
    sine = angle * (1.0 + square * (-1.0 / 6 + square * (1.0 / 120 + square * (-1.0 / 5040 + square * (1.0 / 362880)))))
    cosine = 1.0 + square * (-0.5 + square * (1.0 / 24 + square * (-1.0 / 720 + square * (1.0 / 40320))))
    odd = (turns == 1) | (turns == 3)
    first, second = jnp.where(odd, sine, cosine), jnp.where(odd, cosine, sine)
    return (
        jnp.where((turns == 1) | (turns == 2), -first, first),
        jnp.where((turns == 2) | (turns == 3), -second, second),
    )


def fill_table(chan_ref, table_ref, frame_len):
    slots = chan_ref.shape[0]
    norm_scale = 1.0 / math.sqrt(frame_len)

    def block(step, carry):
        rows = pl.ds(pl.multiple_of(step * 64, 64), 64)
        lane = lax.broadcasted_iota(jnp.int32, (64, LANES), 1)
        channels = chan_ref[rows, :]
        fine_cos, fine_sin = turn_of(lax.rem(channels * lane, frame_len), frame_len)
        coarse_cos, coarse_sin = turn_of(lax.rem(channels * lane * LANES, frame_len), frame_len)
        coarse_cos, coarse_sin = coarse_cos * norm_scale, coarse_sin * norm_scale
        for part in range(frame_len // LANES):
            span = pl.ds(part * LANES, LANES)
            cosine, sine = coarse_cos[:, part : part + 1], coarse_sin[:, part : part + 1]
            below = pl.ds(pl.multiple_of(slots + step * 64, 64), 64)
            table_ref[rows, span] = (cosine * fine_cos - sine * fine_sin).astype(table_ref.dtype)
            table_ref[below, span] = -(sine * fine_cos + cosine * fine_sin).astype(table_ref.dtype)
        return carry

    lax.fori_loop(0, slots // 64, block, 0)


def transform_kernel(row_first, rows, nexts, starts, owners, cores, *refs):
    place_ref, good_ref, flag_ref, volt_ref, coef_ref, table_in, _, *refs = refs
    if starts:
        table_out, *refs = refs
    out_refs = refs[: BLOCKS if owners else 1]
    index_ref, raw, wide, hot, weight, filt, turn, table, sems, table_sem = refs[len(out_refs) :]
    taps, frame_len = coef_ref.shape
    ins = flag_ref.shape[0]
    blocks = BLOCKS
    block_len = good_ref.shape[0] // BLOCKS
    slots = table.shape[0] // 2
    ring, ahead = wide.shape[0], raw.shape[0]
    pairs = rows * ins // LANES
    block = place_ref[0]

    if starts:
        move = pltpu.make_async_copy(table, table_out, table_sem)
    else:
        move = pltpu.make_async_copy(table_in, table, table_sem)
        move.start()

    def note(s, carry):
        seen, latest = carry
        if nexts:
            keep = (block + 1 < blocks) & (good_ref[jnp.minimum(block + 1, blocks - 1) * block_len + s] > 0)
        else:
            keep = good_ref[block * block_len + s] > 0
        mine = keep & (seen >= row_first) & (seen < row_first + rows)
        spectrum = s + block_len if nexts else s

        @pl.when(mine)
        def _():
            index_ref[seen - row_first] = spectrum

        return seen + keep.astype(jnp.int32), jnp.where(mine, spectrum, latest)

    span = taps - 1 if nexts else block_len
    seen, latest = lax.fori_loop(0, span, note, (jnp.int32(0), jnp.int32(block_len - 1)))
    used = jnp.clip(seen - row_first, 0, rows)

    def rest(r, carry):
        index_ref[r] = latest
        return carry

    lax.fori_loop(used, rows, rest, 0)
    first = index_ref[0]
    end = index_ref[rows - 1] + taps

    def inside(extended):
        return (extended >= taps - 1) & (extended < taps - 1 + block_len)

    def on_copy(extended):
        slot = lax.rem(extended, ahead)
        begin = pl.multiple_of((extended - (taps - 1)) * frame_len, frame_len)
        return pltpu.make_async_copy(volt_ref.at[:, pl.ds(begin, frame_len)], raw.at[slot], sems.at[slot])

    def fetch(extended):
        @pl.when((extended < end) & inside(extended))
        def _():
            on_copy(extended).start()

    for k in range(ahead):
        fetch(first + k)
    if starts:
        fill_table(table_in, table, frame_len)
        move.start()

    spectrum = lax.broadcasted_iota(jnp.int32, (1, hot.shape[1]), 1) + (block_len if nexts else 0)
    for r in range(rows):
        chosen = (spectrum == index_ref[r]) & (jnp.int32(r) < used)
        hot[pl.ds((r % 2) * (rows // 2) + r // 2, 1), :] = chosen.astype(jnp.float32)
    flags = flag_ref[...].astype(jnp.float32)
    weights = lax.dot_general(hot[...], flags, (((1,), (1,)), ((), ())), preferred_element_type=jnp.float32)
    weight[...] = jnp.concatenate([weights[: rows // 2], weights[rows // 2 :]], axis=1)

    def take(extended, carry):
        to, came = lax.rem(extended, ring), lax.rem(extended, ahead)

        @pl.when(inside(extended))
        def _():
            on_copy(extended).wait()
            for col in range(frame_len // LANES):
                wide[to, col] = raw[came, :, col * LANES : (col + 1) * LANES].astype(jnp.float32)

        @pl.when(jnp.logical_not(inside(extended)))
        def _():
            wide[to] = jnp.zeros(wide.shape[1:], wide.dtype)

        fetch(extended + ahead)
        return carry

    def filter_row(r, have):
        base = index_ref[r]
        lax.fori_loop(have, base + taps, take, 0)
        places = [lax.rem(base + k, ring) for k in range(taps)]
        at = pl.ds(pl.multiple_of(r * ins, ins), ins)
        for col in range(frame_len // LANES):
            here = pl.ds(col * LANES, LANES)
            total = None
            for k in range(taps):
                term = wide[places[k], col] * coef_ref[pl.ds(k, 1), here]
                total = term if total is None else total + term
            filt[at, here] = total.astype(jnp.bfloat16)
        return jnp.maximum(have, base + taps)

    lax.fori_loop(0, rows, filter_row, first)
    if not starts:
        move.wait()
    per_dot = COLS // LANES
    high = 2 * COLS

    def multiply(n, carry):
        for cut in range(2 * slots // high):
            spec = lax.dot_general(
                table[cut * high : (cut + 1) * high, :],
                filt[pl.ds(pl.multiple_of(n * COLS, COLS), COLS), :],
                (((1,), (1,)), ((), ())),
                preferred_element_type=jnp.float32,
            )
            for h in range(per_dot):
                b = n * per_dot + h
                turn[pl.ds(pl.multiple_of(b * 2 * slots + cut * high, high), high), :] = (
                    spec[:, h * LANES : (h + 1) * LANES] * weight[pl.ds(b, 1), :]
                )
        return carry

    lax.fori_loop(0, pairs // per_dot, multiply, 0)

    def corner(out_ref, slot, at):
        real = turn[pl.ds(slot, pairs, stride=2 * slots), :]
        imag = turn[pl.ds(slots + slot, pairs, stride=2 * slots), :]
        out_ref[at] = jnp.concatenate([real, imag], axis=0).astype(jnp.bfloat16)

    def corners(out_ref, begin, at, count):
        def some(j, carry):
            for u in range(8):
                corner(out_ref, begin + j * 8 + u, at + j * 8 + u)
            return carry

        lax.fori_loop(0, count // 8, some, 0)

    if owners:
        own = out_refs[0].shape[0] // (owners // BLOCKS)
        for way in range(owners // BLOCKS):
            for other in range(BLOCKS):
                target = lax.rem(block + other, BLOCKS)
                begin = ((way // cores * BLOCKS + target) * cores + way % cores) * own
                corners(out_refs[other], begin, way * own, own)
    else:
        corners(out_refs[0], 0, 0, slots)
    if starts:
        move.wait()


def transform(place, spec_good, flags, voltages, coefs, table, after, row_first, rows, nexts=False, owners=0, cores=0):
    ins = flags.shape[0]
    taps, frame_len = coefs.shape
    starts = table.shape[1] == 1
    slots = table.shape[0] if starts else table.shape[0] // 2
    pairs = rows * ins // LANES
    flops = 2 * rows * ins * frame_len * 2 * slots
    smem = pl.BlockSpec(memory_space=pltpu.SMEM)
    vmem = pl.BlockSpec(memory_space=pltpu.VMEM)
    hbm = pl.BlockSpec(memory_space=pl.ANY)
    out_shape, out_specs = [], []
    if starts:
        out_shape.append(jax.ShapeDtypeStruct((2 * slots, frame_len), jnp.bfloat16))
        out_specs.append(hbm)
    if owners:
        out_shape += [jax.ShapeDtypeStruct((slots // BLOCKS, 2 * pairs, LANES), jnp.bfloat16)] * BLOCKS
    else:
        out_shape.append(jax.ShapeDtypeStruct((slots, 2 * pairs, LANES), jnp.bfloat16))
    out_specs += [vmem] * (len(out_shape) - len(out_specs))
    return pl.pallas_call(
        functools.partial(transform_kernel, row_first, rows, nexts, starts, owners, cores),
        out_shape=out_shape,
        in_specs=[smem, smem, vmem, hbm, vmem, vmem if starts else hbm, hbm],
        out_specs=out_specs,
        scratch_shapes=[
            pltpu.SMEM((rows,), jnp.int32),
            pltpu.VMEM((AHEAD, ins, frame_len), jnp.bfloat16),
            pltpu.VMEM((taps, frame_len // LANES, ins, LANES), jnp.float32),
            pltpu.VMEM((rows, flags.shape[1]), jnp.float32),
            pltpu.VMEM((pairs, LANES), jnp.float32),
            pltpu.VMEM((rows * ins, frame_len), jnp.bfloat16),
            pltpu.VMEM((pairs * 2 * slots, LANES), jnp.float32),
            pltpu.VMEM((2 * slots, frame_len), jnp.bfloat16),
            pltpu.SemaphoreType.DMA((AHEAD,)),
            pltpu.SemaphoreType.DMA,
        ],
        compiler_params=pltpu.CompilerParams(vmem_limit_bytes=VMEM_BYTES),
        cost_estimate=pl.CostEstimate(flops=8 * flops, bytes_accessed=12 * 2**20, transcendentals=0),
        name="filter_transform",
    )(place, spec_good, flags, voltages, coefs, table, voltages if after is None else after)


def correlate_kernel(chips, cores, pieces, *refs):
    scale_ref, refs = refs[0], refs[1:]
    part_refs = refs[:pieces]
    out_ref, straight, turned = refs[-3:]
    ins = LANES // cores
    total = straight.shape[1]
    half = total // 2
    scale = scale_ref[0]
    upper = lax.broadcasted_iota(jnp.int32, (half, half), 1) >= lax.broadcasted_iota(jnp.int32, (half, half), 0)

    def one_slot(slot, carry):
        for chip in range(chips):
            lanes = pl.ds(chip * LANES, LANES)
            place = 0
            for part in part_refs:
                columns = part.shape[0] // (chips * cores)
                depth = part.shape[2]
                half_depth = depth // 2
                low = lax.broadcasted_iota(jnp.int32, (depth, LANES), 1) < ins
                for column in range(columns):
                    sources = [(chip * columns + column) * cores + core for core in range(cores)]
                    one, two = (part[source, slot].astype(jnp.float32) for source in sources)
                    first = jnp.where(low, one, pltpu.roll(two, ins, 1))
                    second = jnp.where(low, pltpu.roll(one, ins, 1), two)
                    for both in (first, second):
                        rows = pl.ds(place, depth)
                        straight[rows, lanes] = both.astype(jnp.bfloat16)
                        turned[rows, lanes] = jnp.concatenate([-both[half_depth:], both[:half_depth]], axis=0).astype(jnp.bfloat16)
                        place += depth
        left = straight[...].T

        def product(a, ref, b):
            return jnp.dot(left[a * half : (a + 1) * half], ref[:, b * half : (b + 1) * half], preferred_element_type=jnp.float32) * scale

        for a in range(2):
            here = pl.ds(a * half, half)
            both = jnp.where(upper, product(a, straight, a), product(a, turned, a))
            out_ref[slot, here, here] = both.astype(out_ref.dtype)
        out_ref[slot, :half, half:] = product(0, straight, 1).astype(out_ref.dtype)
        out_ref[slot, half:, :half] = product(1, turned, 0).astype(out_ref.dtype)
        return carry

    lax.fori_loop(0, out_ref.shape[0], one_slot, 0, unroll=2)


def correlate(scale, parts, into, first, own, chips, cores):
    count = min(part.shape[1] - begin for part, begin in parts)
    total = chips * LANES
    depth = sum(part.shape[0] // chips * part.shape[2] for part, _ in parts)

    def spec(part, begin):
        return pl.BlockSpec((part.shape[0], SLOTS) + part.shape[2:], lambda c: (0, c + begin // SLOTS, 0, 0))

    arrays = [part for part, _ in parts]
    in_specs = [pl.BlockSpec(memory_space=pltpu.SMEM)] + [spec(*pair) for pair in parts]
    operands = [scale] + arrays
    aliases = {}
    kernel = functools.partial(correlate_kernel, chips, cores, len(parts))
    if into is not None:
        aliases = {len(operands): 0}
        operands.append(into)
        in_specs.append(pl.BlockSpec(memory_space=pl.ANY))
    return pl.pallas_call(
        kernel,
        grid=(count // SLOTS,),
        out_shape=jax.ShapeDtypeStruct((own, total, total), jnp.bfloat16),
        in_specs=in_specs,
        out_specs=pl.BlockSpec((SLOTS, total, total), lambda c: (c + first // SLOTS, 0, 0)),
        scratch_shapes=[pltpu.VMEM((depth, total), jnp.bfloat16)] * 2,
        input_output_aliases=aliases,
        compiler_params=pltpu.CompilerParams(vmem_limit_bytes=VMEM_BYTES),
        cost_estimate=pl.CostEstimate(
            flops=count * 8 * total * total * depth, bytes_accessed=count * 3 * total * total, transcendentals=0
        ),
        name="correlate",
    )(*operands)


def make_plain_table(channels, frame_len):
    samples = jnp.arange(frame_len, dtype=jnp.int32)
    phase_index = samples[:, None] * channels[None, :] % frame_len
    angles = phase_index.astype(jnp.float32) * (2.0 * math.pi / frame_len)
    norm_scale = 1.0 / math.sqrt(frame_len)
    return jnp.stack([jnp.cos(angles) * norm_scale, -jnp.sin(angles) * norm_scale], axis=1).astype(
        jnp.bfloat16
    )


def correlate_one(spectra_block):
    input_total = spectra_block.shape[0]
    half_width = spectra_block.shape[1] // 2
    rotated = jnp.concatenate(
        [spectra_block[:, half_width:], -spectra_block[:, :half_width]], axis=1
    )
    stacked = jnp.concatenate([spectra_block, rotated], axis=0)
    products = jnp.dot(stacked, spectra_block.T, preferred_element_type=jnp.float32)
    upper_mask = jnp.arange(input_total)[None, :] >= jnp.arange(input_total)[:, None]
    return jnp.where(upper_mask, products[:input_total], products[input_total:])


def rounded(values):
    return lax.optimization_barrier(values.astype(jnp.bfloat16)).astype(jnp.float32)


def local_plain(voltages, pfb_coeffs, input_flags, spec_good, chan_map):
    tap_count, frame_len = pfb_coeffs.shape
    local_inputs, block_len = input_flags.shape
    frames = voltages.reshape(local_inputs, block_len, frame_len)
    earlier = passed_along(frames[:, block_len - tap_count + 1 :, :], "tblk", 1)
    extended = jnp.concatenate([earlier, frames], axis=1)
    summed = jnp.zeros((local_inputs, block_len, frame_len), jnp.float32)
    for tap_index in range(tap_count):
        window_part = extended[:, tap_index : tap_index + block_len, :]
        summed = summed + pfb_coeffs[tap_index][None, None, :] * window_part.astype(jnp.float32)
    block_index = lax.axis_index("tblk")
    good_here = lax.dynamic_slice_in_dim(spec_good, block_index * block_len, block_len)
    weights = input_flags * good_here[None, :]
    filtered = (summed * weights.astype(jnp.float32)[:, :, None]).astype(jnp.bfloat16)
    inp_count = lax.axis_size("inp")
    tblk_count = lax.axis_size("tblk")
    sub_count = lax.axis_size("sub")
    chan_total = chan_map.shape[0]
    per_owner = chan_total // (inp_count * tblk_count * sub_count)
    live_total = jnp.sum(spec_good).astype(jnp.float32)
    slot_order = jnp.arange(chan_total).reshape(inp_count, tblk_count, sub_count, per_owner)
    slot_order = slot_order.transpose(0, 2, 1, 3).reshape(chan_total)
    dft_table = make_plain_table(chan_map[slot_order], frame_len)
    spectra = jnp.einsum("isn,nqj->jiqs", filtered, dft_table, preferred_element_type=jnp.float32)
    spectra = spectra.astype(jnp.bfloat16).reshape(chan_total, local_inputs, -1)
    turned = lax.all_to_all(spectra, ("inp", "sub"), split_axis=0, concat_axis=1, tiled=True)
    summed_vis = lax.psum_scatter(
        rounded(lax.map(correlate_one, turned)).astype(jnp.bfloat16),
        "tblk",
        scatter_dimension=0,
        tiled=True,
    ).astype(jnp.float32)
    return (summed_vis / live_total).astype(jnp.bfloat16)


def local(voltages, pfb_coeffs, input_flags, spec_good, chan_map):
    taps, frame_len = pfb_coeffs.shape
    ins, block_len = input_flags.shape
    chips, blocks, cores = (lax.axis_size(axis) for axis in ("inp", "tblk", "sub"))
    owners = chips * blocks * cores
    slots = chan_map.shape[0]
    own = slots // owners
    if blocks != BLOCKS or ins * cores != LANES or own % 16 or ins % 16 or slots % 64 or taps > STEP:
        return local_plain(voltages, pfb_coeffs, input_flags, spec_good, chan_map)
    ways = chips * cores
    block = lax.axis_index("tblk").astype(jnp.int32)
    scale = (1.0 / jnp.sum(spec_good).astype(jnp.float32)).reshape(1)
    next_flags = passed_along(input_flags[:, :taps], "tblk", -1)

    def chunk(row_first, rows, table, after, flags=input_flags, **rest):
        return transform(block.reshape(1), spec_good, flags, voltages, pfb_coeffs, table, after, row_first, rows, **rest)

    def swapped(piece):
        return lax.ppermute(piece, "tblk", [(0, 1), (1, 0)])

    def turn(piece, axes, before):
        if before is not None:
            piece, before = lax.optimization_barrier((piece, before))
        return lax.all_to_all(piece, axes, split_axis=0, concat_axis=0, tiled=True), before

    column = ("inp", "sub")
    table, early = chunk(STEP, STEP, chan_map.reshape(slots, 1), None)
    early = early.reshape(owners, own, *early.shape[1:])
    early, _ = turn(early, ("inp", "tblk", "sub"), None)
    split = dict(owners=owners, cores=cores)
    middle = [part.reshape(ways, own, *part.shape[1:]) for part in chunk(2 * STEP, 2 * STEP, table, table, **split)]
    middle_own, early = turn(middle[0], column, early)
    middle_other = swapped(middle[1])
    over = [part.reshape(ways, own, *part.shape[1:]) for part in chunk(0, STEP, table, middle[0], next_flags, nexts=True, **split)]
    late = [part.reshape(ways, own, *part.shape[1:]) for part in chunk(0, STEP, table, over[0], **split)]
    late_other, over_other = swapped(late[1]), swapped(over[1])
    middle_other, late[0] = lax.optimization_barrier((middle_other, late[0]))
    middle_other, middle_own = turn(middle_other, column, middle_own)

    def added(a, b, here):
        return (a.astype(jnp.float32) + jnp.where(here, b.astype(jnp.float32), 0.0)).astype(jnp.bfloat16)

    out, before = None, middle_other
    cut = own * 3 // 4
    tails = []
    for begin, end in ((0, cut), (cut, own)):
        mine = added(late[0][:, begin:end], over_other[:, begin:end], block > 0)
        others = added(late_other[:, begin:end], over[0][:, begin:end], block == 0)
        half = mine.shape[2] // 2
        piece = jnp.concatenate([mine[:, :, :half], others[:, :, :half], mine[:, :, half:], others[:, :, half:]], axis=2)
        tail, before = turn(piece, column, before)
        if tails:
            tails[0] = before
        else:
            middle_other = before
        tails.append(tail)
        before = tail
    for (begin, end), tail in zip(((0, cut), (cut, own)), tails):
        parts = [(early, begin), (middle_own, begin), (middle_other, begin), (tail, 0)]
        out = correlate(scale, parts, out, begin, own, chips, cores)
    return out


def solution(mesh):
    return jax.shard_map(
        local,
        mesh=mesh,
        in_specs=(
            P(("grp", "inp", "sub"), "tblk"),
            P(),
            P(("grp", "inp", "sub"), "tblk"),
            P("grp"),
            P(),
        ),
        out_specs=P(("grp", "inp", "tblk", "sub"), None, None),
        check_vma=False,
    )
```

time: 443 us -> 270 us (0.61)
  Pallas kernels: 226 us -> 142 us
  waiting for transfers between devices: 126 us -> 79.1 us
  blocking collectives: 44.4 us -> 0 us
  other arithmetic: 0.63 us -> 8.22 us
    pallas_call x5 -> x6, Pallas kernels: 226 us -> 142 us  [the longest x4 122 us: transform(): pl.pallas_call(functools.partial(transform_kernel, row_first, rows, nexts...]
    ppermute x1, waiting for transfers between devices: 51.8 us -> 0.01 us  [passed_along(): lax.ppermute(value, axis, [(source, source + steps) for source in range(i...]
    all_to_all x1 -> x0, blocking collectives: 44.4 us -> none  [turn(): lax.all_to_all(piece, ('inp', 'tblk', 'sub'), split_axis=0, concat_axis=0...]
    ppermute x0 -> x3, waiting for transfers between devices: none -> 44.4 us  [swapped(): return lax.ppermute(piece, 'tblk', [(0, 1), (1, 0)])]
    all_to_all x3 -> x5, waiting for transfers between devices: 74.5 us -> 34.7 us  [turn(): lax.all_to_all(piece, axes, split_axis=0, concat_axis=0, tiled=True)]
    ppermute x1, starting transfers between devices: 6.79 us -> 1.28 us  [passed_along(): lax.ppermute(value, axis, [(source, source + steps) for source in range(i...]
    ppermute x0 -> x3, starting transfers between devices: none -> 5.49 us  [swapped(): return lax.ppermute(piece, 'tblk', [(0, 1), (1, 0)])]
    convert_element_type x0 -> x4, other arithmetic: none -> 5.19 us  [added(): (a.astype(jnp.float32) + jnp.where(here, b.astype(jnp.float32), 0.0)).ast...]
  transfers between devices with their start and end apart: 4 -> 9, of which waited for: 2 -> 4; matrix products, arithmetic and copies ran while one was open for 1% -> 4% of each run, Pallas kernels for 21% -> 50%
where the time goes in v3:
time: 270 us; the launch traced here: 269 us
  Pallas kernels  142 us (53%)
  waiting for transfers between devices  79.1 us (29%)
  starting transfers between devices  34 us (13%)
  other arithmetic  8.22 us (3%)
  local copies, waits for them, and re-layouts  4.76 us (2%)
    pallas_call x4, Pallas kernels, transform(): pl.pallas_call(functools.partial(transform_kernel, row_first, rows, nexts...  122 us
    ppermute x3, waiting for transfers between devices, swapped(): return lax.ppermute(piece, 'tblk', [(0, 1), (1, 0)])  44.4 us
    all_to_all x5, waiting for transfers between devices, turn(): lax.all_to_all(piece, axes, split_axis=0, concat_axis=0, tiled=True)  34.7 us
    all_to_all x5, starting transfers between devices, turn(): lax.all_to_all(piece, axes, split_axis=0, concat_axis=0, tiled=True)  27.3 us
    pallas_call x2, Pallas kernels, correlate(): pl.pallas_call(kernel, grid=(count // SLOTS,), out_shape=jax.ShapeDtypeSt...  20.1 us
    ppermute x3, starting transfers between devices, swapped(): return lax.ppermute(piece, 'tblk', [(0, 1), (1, 0)])  5.49 us
  transfers between devices with their start and end apart: 9, of which 4 were waited for; matrix products, arithmetic and copies ran while one was open for 4% of the time, Pallas kernels for 50%

profile of v3, /device:TPU:0, one launch (start us, length us, event | category | flops | bytes accessed | tf_op | source)
XLA Modules:
  0.0 268.9 jit_solution(18385859599552454831)
XLA Ops:
  0.0 1.3 collective-permute-start.1
  1.3 1.5 copy.7.refs_5_
  2.8 30.4 %filter_transform.4 = (bf16[1024,2048]{1,0:T(8,128)(2,1)}, bf16[512,16,128]{2,1,0:T(8,128)(2,1)}) custom-call(s32[1]{0:T(128)} %bitcast.1.refs_0_, s32[192]{0:T(256)} %refs_1_.7, s32[64,96]{1,0:T(8,128)} %refs_2_.5, bf16[64,196608]{1,0:T(8,128)(2,1)} %refs_3_.7, f32[16,2048]{1,0:T(8,128)} %refs_4_.7, s32[512,1]{1,0:T(8,128)} %copy.7.refs_5_, ...), custom_call_target="tpu_custom_call" | custom-call | flops 34359738368 | bytes 12582912 | tf_op jit(solution)/shard_map/filter_transform/pallas_call | solution.py:237
  33.2 8.0 %all-to-all-start = ((bf16[16,32,16,128]{3,2,1,0:T(8,128)(2,1)}), bf16[16,32,16,128]{3,2,1,0:T(8,128)(2,1)S(1)}, u32[]{:S(2)}, u32[]{:S(2)}) async-start(bf16[16,32,16,128]{3,2,1,0:T(8,128)(2,1)} %bitcast.13), calls=%async_computation | async-start | bytes 4194304 | tf_op jit(solution)/shard_map/all_to_all | solution.py:422
  41.3 42.7 %filter_transform.5 = (bf16[256,32,128]{2,1,0:T(8,128)(2,1)}, bf16[256,32,128]{2,1,0:T(8,128)(2,1)}) custom-call(s32[1]{0:T(128)} %bitcast.1.refs_0_, s32[192]{0:T(256)} %refs_1_.7, s32[64,96]{1,0:T(8,128)} %refs_2_.5, bf16[64,196608]{1,0:T(8,128)(2,1)} %refs_3_.7, f32[16,2048]{1,0:T(8,128)} %refs_4_.7, ...), custom_call_target="tpu_custom_call" | custom-call | flops 68719476736 | bytes 12582912 | tf_op jit(solution)/shard_map/filter_transform/pallas_call | solution.py:237
  84.0 3.4 %collective-permute-start = (bf16[8,32,32,128]{3,2,1,0:T(8,128)(2,1)}, bf16[8,32,32,128]{3,2,1,0:T(8,128)(2,1)}, u32[]{:S(2)}, u32[]{:S(2)}) collective-permute-start(bf16[8,32,32,128]{3,2,1,0:T(8,128)(2,1)} %bitcast.20), channel_id=1, source_target_pairs={{0,2},{2,0},{1,3},{3,1},{4,6},{6,4},{5,7},{7,5},{8,10},{10,8},{9,1... | collective-permute-start | bytes 6291464 | tf_op jit(solution)/shard_map/ppermute | solution.py:417
  87.4 1.3 copy-done
  88.7 5.7 %all-to-all-start.1 = ((bf16[8,32,32,128]{3,2,1,0:T(8,128)(2,1)}), bf16[8,32,32,128]{3,2,1,0:T(8,128)(2,1)}, u32[]{:S(2)}, u32[]{:S(2)}) async-start(bf16[8,32,32,128]{3,2,1,0:T(8,128)(2,1)} %bitcast.11), calls=%async_computation.1 | async-start | bytes 4194304 | tf_op jit(solution)/shard_map/all_to_all | solution.py:422
  94.4 0.6 copy-done.5
  95.0 24.3 %filter_transform.6 = (bf16[256,16,128]{2,1,0:T(8,128)(2,1)}, bf16[256,16,128]{2,1,0:T(8,128)(2,1)}) custom-call(s32[1]{0:T(128)} %bitcast.1.refs_0_, s32[192]{0:T(256)} %refs_1_.7, s32[64,16]{1,0:T(8,128)} %copy-done.5, bf16[64,196608]{1,0:T(8,128)(2,1)} %refs_3_.7, f32[16,2048]{1,0:T(8,128)} %refs_4_.7, ...), custom_call_target="tpu_custom_call" | custom-call | flops 34359738368 | bytes 12582912 | tf_op jit(solution)/shard_map/filter_transform/pallas_call | solution.py:237
  119.3 24.4 %filter_transform.7 = (bf16[256,16,128]{2,1,0:T(8,128)(2,1)}, bf16[256,16,128]{2,1,0:T(8,128)(2,1)}) custom-call(s32[1]{0:T(128)} %bitcast.1.refs_0_, s32[192]{0:T(256)} %refs_1_.7, s32[64,96]{1,0:T(8,128)} %refs_2_.5, bf16[64,196608]{1,0:T(8,128)(2,1)} %refs_3_.7, f32[16,2048]{1,0:T(8,128)} %refs_4_.7, ...), custom_call_target="tpu_custom_call" | custom-call | flops 34359738368 | bytes 12582912 | tf_op jit(solution)/shard_map/filter_transform/pallas_call | solution.py:237
  143.7 5.1 %all-to-all-start.2 = ((bf16[8,32,32,128]{3,2,1,0:T(8,128)(2,1)}), bf16[8,32,32,128]{3,2,1,0:T(8,128)(2,1)S(1)}, u32[]{:S(2)}, u32[]{:S(2)}) async-start(bf16[8,32,32,128]{3,2,1,0:T(8,128)(2,1)} %collective-permute-done), calls=%async_computation.2 | async-start | bytes 4194304 | tf_op jit(solution)/shard_map/all_to_all | solution.py:422
  148.9 0.1 collective-permute-start.3
  148.9 2.0 collective-permute-start.2
  151.0 24.3 %collective-permute-done.3 = bf16[8,32,16,128]{3,2,1,0:T(8,128)(2,1)} collective-permute-done((bf16[8,32,16,128]{3,2,1,0:T(8,128)(2,1)}, bf16[8,32,16,128]{3,2,1,0:T(8,128)(2,1)}, u32[]{:S(2)}, u32[]{:S(2)}) %collective-permute-start.3) | collective-permute-done | bytes 1048608 | tf_op jit(solution)/shard_map/ppermute | solution.py:417
  175.2 1.6 add_convert_fusion
  176.8 0.2 fusion.1
  177.1 20.2 %collective-permute-done.2 = bf16[8,32,16,128]{3,2,1,0:T(8,128)(2,1)} collective-permute-done((bf16[8,32,16,128]{3,2,1,0:T(8,128)(2,1)}, bf16[8,32,16,128]{3,2,1,0:T(8,128)(2,1)}, u32[]{:S(2)}, u32[]{:S(2)}) %collective-permute-start.2) | collective-permute-done | bytes 1048608 | tf_op jit(solution)/shard_map/ppermute | solution.py:417
  197.2 1.4 add_convert_fusion.1
  198.6 0.2 fusion
  198.8 1.4 pad_maximum_fusion
  200.2 4.9 %all-to-all-start.3 = ((bf16[8,24,32,128]{3,2,1,0:T(8,128)(2,1)}), bf16[8,24,32,128]{3,2,1,0:T(8,128)(2,1)}, u32[]{:S(2)}, u32[]{:S(2)}) async-start(bf16[8,24,32,128]{3,2,1,0:T(8,128)(2,1)} %pad_maximum_fusion), calls=%async_computation.3 | async-start | bytes 3145728 | tf_op jit(solution)/shard_map/all_to_all | solution.py:422
  205.1 0.7 reduce_sum.9
  206.5 1.1 add_convert_fusion.2
  207.7 1.0 add_convert_fusion.3
  208.8 0.9 pad_maximum_fusion.1
  209.7 33.3 %all-to-all-done.3.refs_4_ = bf16[8,24,32,128]{3,2,1,0:T(8,128)(2,1)} async-done(((bf16[8,24,32,128]{3,2,1,0:T(8,128)(2,1)}), bf16[8,24,32,128]{3,2,1,0:T(8,128)(2,1)}, u32[]{:S(2)}, u32[]{:S(2)}) %all-to-all-start.3) | async-done | bytes 1572896 | tf_op jit(solution)/shard_map/all_to_all | solution.py:422
  243.1 3.5 %all-to-all-start.4 = ((bf16[8,8,32,128]{3,2,1,0:T(8,128)(2,1)}), bf16[8,8,32,128]{3,2,1,0:T(8,128)(2,1)S(1)}, u32[]{:S(2)}, u32[]{:S(2)}) async-start(bf16[8,8,32,128]{3,2,1,0:T(8,128)(2,1)} %pad_maximum_fusion.1), calls=%async_computation.4 | async-start | bytes 1048576 | tf_op jit(solution)/shard_map/all_to_all | solution.py:422
  246.6 13.9 %correlate.2.refs_5_ = bf16[32,512,512]{2,1,0:T(8,128)(2,1)} custom-call(f32[1]{0:T(128)} %bitcast.refs_0_, bf16[16,32,16,128]{3,2,1,0:T(8,128)(2,1)} %copy-done, bf16[8,32,32,128]{3,2,1,0:T(8,128)(2,1)} %all-to-all-done.1.refs_2_, bf16[8,32,32,128]{3,2,1,0:T(8,128)(2,1)} %copy-done.1, bf16[8,24,32,128]{3,2,1,0:T(8,128)(2,1)} %all-to-all-done.3.refs_4_), custom_call_target="tpu_custom_call" | custom-call | flops 12884901888 | bytes 18874368 | tf_op jit(solution)/shard_map/correlate/pallas_call | solution.py:322
  260.5 1.4 all-to-all-done.4.refs_4_
  261.8 0.8 copy-done.2
  262.6 6.2 %correlate.3 = bf16[32,512,512]{2,1,0:T(8,128)(2,1)} custom-call(f32[1]{0:T(128)} %bitcast.refs_0_, bf16[16,32,16,128]{3,2,1,0:T(8,128)(2,1)} %copy-done, bf16[8,32,32,128]{3,2,1,0:T(8,128)(2,1)} %all-to-all-done.1.refs_2_, bf16[8,32,32,128]{3,2,1,0:T(8,128)(2,1)} %copy-done.1, bf16[8,8,32,128]{3,2,1,0:T(8,128)(2,1)} %copy-done.2, ...), custom_call_target="tpu_custom_call", output_to_operand_aliasing={{}: (5, {})} | custom-call | flops 4294967296 | bytes 6291456 | tf_op jit(solution)/shard_map/correlate/pallas_call | solution.py:322
  (16 shorter events, 0.1 us)
Async XLA Ops:
  0.0 94.4 %collective-permute-start.1 = (s32[64,16]{1,0:T(8,128)}, s32[64,16]{1,0:T(8,128)S(1)}, u32[]{:S(2)}, u32[]{:S(2)}) collective-permute-start(s32[64,16]{1,0:T(8,128)} %bitcast.23), channel_id=1, source_target_pairs={{2,0},{3,1},{6,4},{7,5},{10,8},{11,9},{14,12},{15,13},{18,16},{19,... | collective-permute-start | bytes 12296 | tf_op jit(solution)/shard_map/ppermute | solution.py:24
  33.2 54.2 %all-to-all-start = ((bf16[16,32,16,128]{3,2,1,0:T(8,128)(2,1)}), bf16[16,32,16,128]{3,2,1,0:T(8,128)(2,1)S(1)}, u32[]{:S(2)}, u32[]{:S(2)}) async-start(bf16[16,32,16,128]{3,2,1,0:T(8,128)(2,1)} %bitcast.13), calls=%async_computation | async-start | bytes 4194304 | tf_op jit(solution)/shard_map/all_to_all | solution.py:422
  84.0 59.7 %collective-permute-start = (bf16[8,32,32,128]{3,2,1,0:T(8,128)(2,1)}, bf16[8,32,32,128]{3,2,1,0:T(8,128)(2,1)}, u32[]{:S(2)}, u32[]{:S(2)}) collective-permute-start(bf16[8,32,32,128]{3,2,1,0:T(8,128)(2,1)} %bitcast.20), channel_id=1, source_target_pairs={{0,2},{2,0},{1,3},{3,1},{4,6},{6,4},{5,7},{7,5},{8,10},{10,8},{9,1... | collective-permute-start | bytes 6291464 | tf_op jit(solution)/shard_map/ppermute | solution.py:417
  87.4 1.3 copy-start
  88.7 55.0 %all-to-all-start.1 = ((bf16[8,32,32,128]{3,2,1,0:T(8,128)(2,1)}), bf16[8,32,32,128]{3,2,1,0:T(8,128)(2,1)}, u32[]{:S(2)}, u32[]{:S(2)}) async-start(bf16[8,32,32,128]{3,2,1,0:T(8,128)(2,1)} %bitcast.11), calls=%async_computation.1 | async-start | bytes 4194304 | tf_op jit(solution)/shard_map/all_to_all | solution.py:422
  94.4 0.6 copy-start.5
  143.7 56.5 %all-to-all-start.2 = ((bf16[8,32,32,128]{3,2,1,0:T(8,128)(2,1)}), bf16[8,32,32,128]{3,2,1,0:T(8,128)(2,1)S(1)}, u32[]{:S(2)}, u32[]{:S(2)}) async-start(bf16[8,32,32,128]{3,2,1,0:T(8,128)(2,1)} %collective-permute-done), calls=%async_computation.2 | async-start | bytes 4194304 | tf_op jit(solution)/shard_map/all_to_all | solution.py:422
  148.9 48.4 %copy-start.3 = (bf16[256,16,128]{2,1,0:T(8,128)(2,1)S(1)}, bf16[256,16,128]{2,1,0:T(8,128)(2,1)}, u32[]{:S(2)}) copy-start(bf16[256,16,128]{2,1,0:T(8,128)(2,1)} %get-tuple-element.29) | copy-start | bytes 3145732
  148.9 26.3 %collective-permute-start.3 = (bf16[8,32,16,128]{3,2,1,0:T(8,128)(2,1)}, bf16[8,32,16,128]{3,2,1,0:T(8,128)(2,1)}, u32[]{:S(2)}, u32[]{:S(2)}) collective-permute-start(bf16[8,32,16,128]{3,2,1,0:T(8,128)(2,1)} %bitcast.22), channel_id=1, source_target_pairs={{0,2},{2,0},{1,3},{3,1},{4,6},{6,4},{5,7},{7,5},{8,10},{10,8},{9,1... | collective-permute-start | bytes 3145736 | tf_op jit(solution)/shard_map/ppermute | solution.py:417
  148.9 48.3 %collective-permute-start.2 = (bf16[8,32,16,128]{3,2,1,0:T(8,128)(2,1)}, bf16[8,32,16,128]{3,2,1,0:T(8,128)(2,1)}, u32[]{:S(2)}, u32[]{:S(2)}) collective-permute-start(bf16[8,32,16,128]{3,2,1,0:T(8,128)(2,1)} %bitcast.21), channel_id=1, source_target_pairs={{0,2},{2,0},{1,3},{3,1},{4,6},{6,4},{5,7},{7,5},{8,10},{10,8},{9,1... | collective-permute-start | bytes 3145736 | tf_op jit(solution)/shard_map/ppermute | solution.py:417
  200.2 4.9 %copy-start.4 = (s32[192]{0:T(256)S(1)}, s32[192]{0:T(256)}, u32[]{:S(2)}) copy-start(s32[192]{0:T(256)} %refs_1_.7) | copy-start | bytes 2308
  200.2 7.4 %copy-start.1 = (bf16[8,32,32,128]{3,2,1,0:T(8,128)(2,1)}, bf16[8,32,32,128]{3,2,1,0:T(8,128)(2,1)S(1)}, u32[]{:S(2)}) copy-start(bf16[8,32,32,128]{3,2,1,0:T(8,128)(2,1)S(1)} %all-to-all-done.2.refs_3_) | copy-start | bytes 6291460
  200.2 42.8 %all-to-all-start.3 = ((bf16[8,24,32,128]{3,2,1,0:T(8,128)(2,1)}), bf16[8,24,32,128]{3,2,1,0:T(8,128)(2,1)}, u32[]{:S(2)}, u32[]{:S(2)}) async-start(bf16[8,24,32,128]{3,2,1,0:T(8,128)(2,1)} %pad_maximum_fusion), calls=%async_computation.3 | async-start | bytes 3145728 | tf_op jit(solution)/shard_map/all_to_all | solution.py:422
  243.1 18.8 %all-to-all-start.4 = ((bf16[8,8,32,128]{3,2,1,0:T(8,128)(2,1)}), bf16[8,8,32,128]{3,2,1,0:T(8,128)(2,1)S(1)}, u32[]{:S(2)}, u32[]{:S(2)}) async-start(bf16[8,8,32,128]{3,2,1,0:T(8,128)(2,1)} %pad_maximum_fusion.1), calls=%async_computation.4 | async-start | bytes 1048576 | tf_op jit(solution)/shard_map/all_to_all | solution.py:422
  261.8 0.8 copy-start.2

commit v4 on v3

--- a/solution.py
+++ b/solution.py
@@ -12,9 +12,10 @@
 STEP = 16
 LANES = 128
 COLS = 256
+PAD = 8
 SLOTS = 4
 BLOCKS = 2
-AHEAD = 8
+AHEAD = 16
 VMEM_BYTES = 56 * 1024 * 1024
 
 
@@ -74,6 +75,7 @@
     slots = table.shape[0] // 2
     ring, ahead = wide.shape[0], raw.shape[0]
     pairs = rows * ins // LANES
+    stride = turn.shape[0] // pairs
     block = place_ref[0]
 
     if starts:
@@ -157,13 +159,34 @@
         lax.fori_loop(have, base + taps, take, 0)
         places = [lax.rem(base + k, ring) for k in range(taps)]
         at = pl.ds(pl.multiple_of(r * ins, ins), ins)
-        for col in range(frame_len // LANES):
-            here = pl.ds(col * LANES, LANES)
-            total = None
-            for k in range(taps):
-                term = wide[places[k], col] * coef_ref[pl.ds(k, 1), here]
-                total = term if total is None else total + term
-            filt[at, here] = total.astype(jnp.bfloat16)
+
+        def add_up(begin, stop):
+            for col in range(frame_len // LANES):
+                here = pl.ds(col * LANES, LANES)
+                total = None
+                for k in range(begin, stop):
+                    term = wide[places[k], col] * coef_ref[pl.ds(k, 1), here]
+                    total = term if total is None else total + term
+                filt[at, here] = total.astype(jnp.bfloat16)
+
+        half = taps // 2
+        live = r < used
+        early = (base + half <= taps - 1) if row_first == 0 and not nexts else False
+        late = (base + half >= taps - 1 + block_len) if nexts else False
+
+        @pl.when(live & jnp.logical_not(early | late))
+        def _():
+            add_up(0, taps)
+
+        if row_first == 0 and not nexts:
+            pl.when(live & early)(lambda: add_up(half, taps))
+        if nexts:
+            pl.when(live & late)(lambda: add_up(0, half))
+
+        @pl.when(jnp.logical_not(live))
+        def _():
+            filt[at, :] = jnp.zeros((ins, frame_len), filt.dtype)
+
         return jnp.maximum(have, base + taps)
 
     lax.fori_loop(0, rows, filter_row, first)
@@ -182,7 +205,7 @@
             )
             for h in range(per_dot):
                 b = n * per_dot + h
-                turn[pl.ds(pl.multiple_of(b * 2 * slots + cut * high, high), high), :] = (
+                turn[pl.ds(pl.multiple_of(b * stride + cut * high, 8), high), :] = (
                     spec[:, h * LANES : (h + 1) * LANES] * weight[pl.ds(b, 1), :]
                 )
         return carry
@@ -190,8 +213,8 @@
     lax.fori_loop(0, pairs // per_dot, multiply, 0)
 
     def corner(out_ref, slot, at):
-        real = turn[pl.ds(slot, pairs, stride=2 * slots), :]
-        imag = turn[pl.ds(slots + slot, pairs, stride=2 * slots), :]
+        real = turn[pl.ds(slot, pairs, stride=stride), :]
+        imag = turn[pl.ds(slots + slot, pairs, stride=stride), :]
         out_ref[at] = jnp.concatenate([real, imag], axis=0).astype(jnp.bfloat16)
 
     def corners(out_ref, begin, at, count):
@@ -246,7 +269,7 @@
             pltpu.VMEM((rows, flags.shape[1]), jnp.float32),
             pltpu.VMEM((pairs, LANES), jnp.float32),
             pltpu.VMEM((rows * ins, frame_len), jnp.bfloat16),
-            pltpu.VMEM((pairs * 2 * slots, LANES), jnp.float32),
+            pltpu.VMEM((pairs * (2 * slots + PAD), LANES), jnp.float32),
             pltpu.VMEM((2 * slots, frame_len), jnp.bfloat16),
             pltpu.SemaphoreType.DMA((AHEAD,)),
             pltpu.SemaphoreType.DMA,

time: 270 us -> 265 us (0.981)
  Pallas kernels: 142 us -> 118 us
  starting transfers between devices: 34 us -> 43.4 us
  waiting for transfers between devices: 79.1 us -> 88.2 us
    pallas_call x4, Pallas kernels: 122 us -> 98.2 us  [transform(): pl.pallas_call(functools.partial(transform_kernel, row_first, rows, nexts...]
    all_to_all x5, waiting for transfers between devices: 34.7 us -> 43.8 us  [turn(): lax.all_to_all(piece, axes, split_axis=0, concat_axis=0, tiled=True)]
    ppermute x3, starting transfers between devices: 5.49 us -> 13.3 us  [swapped(): return lax.ppermute(piece, 'tblk', [(0, 1), (1, 0)])]
  transfers between devices with their start and end apart: 9 -> 9, of which waited for: 4 -> 5; matrix products, arithmetic and copies ran while one was open for 4% -> 4% of each run, Pallas kernels for 50% -> 43%
where the time goes in v4:
time: 265 us; the launch traced here: 264 us
  Pallas kernels  118 us (45%)
  waiting for transfers between devices  88.2 us (33%)
  starting transfers between devices  43.4 us (16%)
  other arithmetic  8.22 us (3%)
  local copies, waits for them, and re-layouts  4.76 us (2%)
    pallas_call x4, Pallas kernels, transform(): pl.pallas_call(functools.partial(transform_kernel, row_first, rows, nexts...  98.2 us
    ppermute x3, waiting for transfers between devices, swapped(): return lax.ppermute(piece, 'tblk', [(0, 1), (1, 0)])  44.3 us
    all_to_all x5, waiting for transfers between devices, turn(): lax.all_to_all(piece, axes, split_axis=0, concat_axis=0, tiled=True)  43.8 us
    all_to_all x5, starting transfers between devices, turn(): lax.all_to_all(piece, axes, split_axis=0, concat_axis=0, tiled=True)  28.8 us
    pallas_call x2, Pallas kernels, correlate(): pl.pallas_call(kernel, grid=(count // SLOTS,), out_shape=jax.ShapeDtypeSt...  20.1 us
    ppermute x3, starting transfers between devices, swapped(): return lax.ppermute(piece, 'tblk', [(0, 1), (1, 0)])  13.3 us
  transfers between devices with their start and end apart: 9, of which 5 were waited for; matrix products, arithmetic and copies ran while one was open for 4% of the time, Pallas kernels for 43%

profile of v4, /device:TPU:0, one launch (start us, length us, event | category | flops | bytes accessed | tf_op | source)
XLA Modules:
  0.0 263.7 jit_solution(7687537008830424042)
XLA Ops:
  0.0 1.3 collective-permute-start.1
  1.3 1.5 copy.7.refs_5_
  2.8 27.3 %filter_transform.4 = (bf16[1024,2048]{1,0:T(8,128)(2,1)}, bf16[512,16,128]{2,1,0:T(8,128)(2,1)}) custom-call(s32[1]{0:T(128)} %bitcast.1.refs_0_, s32[192]{0:T(256)} %refs_1_.7, s32[64,96]{1,0:T(8,128)} %refs_2_.5, bf16[64,196608]{1,0:T(8,128)(2,1)} %refs_3_.7, f32[16,2048]{1,0:T(8,128)} %refs_4_.7, s32[512,1]{1,0:T(8,128)} %copy.7.refs_5_, ...), custom_call_target="tpu_custom_call" | custom-call | flops 34359738368 | bytes 12582912 | tf_op jit(solution)/shard_map/filter_transform/pallas_call | solution.py:260
  30.1 7.7 %all-to-all-start = ((bf16[16,32,16,128]{3,2,1,0:T(8,128)(2,1)}), bf16[16,32,16,128]{3,2,1,0:T(8,128)(2,1)S(1)}, u32[]{:S(2)}, u32[]{:S(2)}) async-start(bf16[16,32,16,128]{3,2,1,0:T(8,128)(2,1)} %bitcast.13), calls=%async_computation | async-start | bytes 4194304 | tf_op jit(solution)/shard_map/all_to_all | solution.py:445
  37.8 31.5 %filter_transform.5 = (bf16[256,32,128]{2,1,0:T(8,128)(2,1)}, bf16[256,32,128]{2,1,0:T(8,128)(2,1)}) custom-call(s32[1]{0:T(128)} %bitcast.1.refs_0_, s32[192]{0:T(256)} %refs_1_.7, s32[64,96]{1,0:T(8,128)} %refs_2_.5, bf16[64,196608]{1,0:T(8,128)(2,1)} %refs_3_.7, f32[16,2048]{1,0:T(8,128)} %refs_4_.7, ...), custom_call_target="tpu_custom_call" | custom-call | flops 68719476736 | bytes 12582912 | tf_op jit(solution)/shard_map/filter_transform/pallas_call | solution.py:260
  69.3 11.2 %collective-permute-start = (bf16[8,32,32,128]{3,2,1,0:T(8,128)(2,1)}, bf16[8,32,32,128]{3,2,1,0:T(8,128)(2,1)}, u32[]{:S(2)}, u32[]{:S(2)}) collective-permute-start(bf16[8,32,32,128]{3,2,1,0:T(8,128)(2,1)} %bitcast.20), channel_id=1, source_target_pairs={{0,2},{2,0},{1,3},{3,1},{4,6},{6,4},{5,7},{7,5},{8,10},{10,8},{9,1... | collective-permute-start | bytes 6291464 | tf_op jit(solution)/shard_map/ppermute | solution.py:440
  80.5 1.3 copy-done
  81.8 9.2 %all-to-all-start.1 = ((bf16[8,32,32,128]{3,2,1,0:T(8,128)(2,1)}), bf16[8,32,32,128]{3,2,1,0:T(8,128)(2,1)}, u32[]{:S(2)}, u32[]{:S(2)}) async-start(bf16[8,32,32,128]{3,2,1,0:T(8,128)(2,1)} %bitcast.11), calls=%async_computation.1 | async-start | bytes 4194304 | tf_op jit(solution)/shard_map/all_to_all | solution.py:445
  91.0 0.6 copy-done.5
  91.6 18.0 %filter_transform.6 = (bf16[256,16,128]{2,1,0:T(8,128)(2,1)}, bf16[256,16,128]{2,1,0:T(8,128)(2,1)}) custom-call(s32[1]{0:T(128)} %bitcast.1.refs_0_, s32[192]{0:T(256)} %refs_1_.7, s32[64,16]{1,0:T(8,128)} %copy-done.5, bf16[64,196608]{1,0:T(8,128)(2,1)} %refs_3_.7, f32[16,2048]{1,0:T(8,128)} %refs_4_.7, ...), custom_call_target="tpu_custom_call" | custom-call | flops 34359738368 | bytes 12582912 | tf_op jit(solution)/shard_map/filter_transform/pallas_call | solution.py:260
  109.5 21.5 %filter_transform.7 = (bf16[256,16,128]{2,1,0:T(8,128)(2,1)}, bf16[256,16,128]{2,1,0:T(8,128)(2,1)}) custom-call(s32[1]{0:T(128)} %bitcast.1.refs_0_, s32[192]{0:T(256)} %refs_1_.7, s32[64,96]{1,0:T(8,128)} %refs_2_.5, bf16[64,196608]{1,0:T(8,128)(2,1)} %refs_3_.7, f32[16,2048]{1,0:T(8,128)} %refs_4_.7, ...), custom_call_target="tpu_custom_call" | custom-call | flops 34359738368 | bytes 12582912 | tf_op jit(solution)/shard_map/filter_transform/pallas_call | solution.py:260
  131.0 9.1 %all-to-all-done.1.refs_2_ = bf16[8,32,32,128]{3,2,1,0:T(8,128)(2,1)} async-done(((bf16[8,32,32,128]{3,2,1,0:T(8,128)(2,1)}), bf16[8,32,32,128]{3,2,1,0:T(8,128)(2,1)}, u32[]{:S(2)}, u32[]{:S(2)}) %all-to-all-start.1) | async-done | bytes 2097184 | tf_op jit(solution)/shard_map/all_to_all | solution.py:445
  140.1 3.6 %all-to-all-start.2 = ((bf16[8,32,32,128]{3,2,1,0:T(8,128)(2,1)}), bf16[8,32,32,128]{3,2,1,0:T(8,128)(2,1)S(1)}, u32[]{:S(2)}, u32[]{:S(2)}) async-start(bf16[8,32,32,128]{3,2,1,0:T(8,128)(2,1)} %collective-permute-done), calls=%async_computation.2 | async-start | bytes 4194304 | tf_op jit(solution)/shard_map/all_to_all | solution.py:445
  143.7 1.1 collective-permute-start.3
  144.8 1.0 collective-permute-start.2
  145.8 24.3 %collective-permute-done.3 = bf16[8,32,16,128]{3,2,1,0:T(8,128)(2,1)} collective-permute-done((bf16[8,32,16,128]{3,2,1,0:T(8,128)(2,1)}, bf16[8,32,16,128]{3,2,1,0:T(8,128)(2,1)}, u32[]{:S(2)}, u32[]{:S(2)}) %collective-permute-start.3) | collective-permute-done | bytes 1048608 | tf_op jit(solution)/shard_map/ppermute | solution.py:440
  170.1 1.6 add_convert_fusion
  171.7 0.2 fusion.1
  171.9 20.1 %collective-permute-done.2 = bf16[8,32,16,128]{3,2,1,0:T(8,128)(2,1)} collective-permute-done((bf16[8,32,16,128]{3,2,1,0:T(8,128)(2,1)}, bf16[8,32,16,128]{3,2,1,0:T(8,128)(2,1)}, u32[]{:S(2)}, u32[]{:S(2)}) %collective-permute-start.2) | collective-permute-done | bytes 1048608 | tf_op jit(solution)/shard_map/ppermute | solution.py:440
  192.0 1.4 add_convert_fusion.1
  193.6 1.4 pad_maximum_fusion
  195.0 4.9 %all-to-all-start.3 = ((bf16[8,24,32,128]{3,2,1,0:T(8,128)(2,1)}), bf16[8,24,32,128]{3,2,1,0:T(8,128)(2,1)}, u32[]{:S(2)}, u32[]{:S(2)}) async-start(bf16[8,24,32,128]{3,2,1,0:T(8,128)(2,1)} %pad_maximum_fusion), calls=%async_computation.3 | async-start | bytes 3145728 | tf_op jit(solution)/shard_map/all_to_all | solution.py:445
  199.9 0.7 reduce_sum.9
  201.3 1.1 add_convert_fusion.2
  202.5 1.0 add_convert_fusion.3
  203.6 0.9 pad_maximum_fusion.1
  204.5 33.3 %all-to-all-done.3.refs_4_ = bf16[8,24,32,128]{3,2,1,0:T(8,128)(2,1)} async-done(((bf16[8,24,32,128]{3,2,1,0:T(8,128)(2,1)}), bf16[8,24,32,128]{3,2,1,0:T(8,128)(2,1)}, u32[]{:S(2)}, u32[]{:S(2)}) %all-to-all-start.3) | async-done | bytes 1572896 | tf_op jit(solution)/shard_map/all_to_all | solution.py:445
  237.8 3.5 %all-to-all-start.4 = ((bf16[8,8,32,128]{3,2,1,0:T(8,128)(2,1)}), bf16[8,8,32,128]{3,2,1,0:T(8,128)(2,1)S(1)}, u32[]{:S(2)}, u32[]{:S(2)}) async-start(bf16[8,8,32,128]{3,2,1,0:T(8,128)(2,1)} %pad_maximum_fusion.1), calls=%async_computation.4 | async-start | bytes 1048576 | tf_op jit(solution)/shard_map/all_to_all | solution.py:445
  241.3 13.9 %correlate.2.refs_5_ = bf16[32,512,512]{2,1,0:T(8,128)(2,1)} custom-call(f32[1]{0:T(128)} %bitcast.refs_0_, bf16[16,32,16,128]{3,2,1,0:T(8,128)(2,1)} %copy-done, bf16[8,32,32,128]{3,2,1,0:T(8,128)(2,1)} %all-to-all-done.1.refs_2_, bf16[8,32,32,128]{3,2,1,0:T(8,128)(2,1)} %copy-done.1, bf16[8,24,32,128]{3,2,1,0:T(8,128)(2,1)} %all-to-all-done.3.refs_4_), custom_call_target="tpu_custom_call" | custom-call | flops 12884901888 | bytes 18874368 | tf_op jit(solution)/shard_map/correlate/pallas_call | solution.py:345
  255.2 1.4 all-to-all-done.4.refs_4_
  256.6 0.8 copy-done.2
  257.4 6.2 %correlate.3 = bf16[32,512,512]{2,1,0:T(8,128)(2,1)} custom-call(f32[1]{0:T(128)} %bitcast.refs_0_, bf16[16,32,16,128]{3,2,1,0:T(8,128)(2,1)} %copy-done, bf16[8,32,32,128]{3,2,1,0:T(8,128)(2,1)} %all-to-all-done.1.refs_2_, bf16[8,32,32,128]{3,2,1,0:T(8,128)(2,1)} %copy-done.1, bf16[8,8,32,128]{3,2,1,0:T(8,128)(2,1)} %copy-done.2, ...), custom_call_target="tpu_custom_call", output_to_operand_aliasing={{}: (5, {})} | custom-call | flops 4294967296 | bytes 6291456 | tf_op jit(solution)/shard_map/correlate/pallas_call | solution.py:345
  (16 shorter events, 0.3 us)
Async XLA Ops:
  0.0 90.9 %collective-permute-start.1 = (s32[64,16]{1,0:T(8,128)}, s32[64,16]{1,0:T(8,128)S(1)}, u32[]{:S(2)}, u32[]{:S(2)}) collective-permute-start(s32[64,16]{1,0:T(8,128)} %bitcast.23), channel_id=1, source_target_pairs={{2,0},{3,1},{6,4},{7,5},{10,8},{11,9},{14,12},{15,13},{18,16},{19,... | collective-permute-start | bytes 12296 | tf_op jit(solution)/shard_map/ppermute | solution.py:25
  30.1 50.4 %all-to-all-start = ((bf16[16,32,16,128]{3,2,1,0:T(8,128)(2,1)}), bf16[16,32,16,128]{3,2,1,0:T(8,128)(2,1)S(1)}, u32[]{:S(2)}, u32[]{:S(2)}) async-start(bf16[16,32,16,128]{3,2,1,0:T(8,128)(2,1)} %bitcast.13), calls=%async_computation | async-start | bytes 4194304 | tf_op jit(solution)/shard_map/all_to_all | solution.py:445
  69.3 61.7 %collective-permute-start = (bf16[8,32,32,128]{3,2,1,0:T(8,128)(2,1)}, bf16[8,32,32,128]{3,2,1,0:T(8,128)(2,1)}, u32[]{:S(2)}, u32[]{:S(2)}) collective-permute-start(bf16[8,32,32,128]{3,2,1,0:T(8,128)(2,1)} %bitcast.20), channel_id=1, source_target_pairs={{0,2},{2,0},{1,3},{3,1},{4,6},{6,4},{5,7},{7,5},{8,10},{10,8},{9,1... | collective-permute-start | bytes 6291464 | tf_op jit(solution)/shard_map/ppermute | solution.py:440
  80.5 1.3 copy-start
  81.8 58.3 %all-to-all-start.1 = ((bf16[8,32,32,128]{3,2,1,0:T(8,128)(2,1)}), bf16[8,32,32,128]{3,2,1,0:T(8,128)(2,1)}, u32[]{:S(2)}, u32[]{:S(2)}) async-start(bf16[8,32,32,128]{3,2,1,0:T(8,128)(2,1)} %bitcast.11), calls=%async_computation.1 | async-start | bytes 4194304 | tf_op jit(solution)/shard_map/all_to_all | solution.py:445
  90.9 0.6 copy-start.5
  140.1 54.9 %all-to-all-start.2 = ((bf16[8,32,32,128]{3,2,1,0:T(8,128)(2,1)}), bf16[8,32,32,128]{3,2,1,0:T(8,128)(2,1)S(1)}, u32[]{:S(2)}, u32[]{:S(2)}) async-start(bf16[8,32,32,128]{3,2,1,0:T(8,128)(2,1)} %collective-permute-done), calls=%async_computation.2 | async-start | bytes 4194304 | tf_op jit(solution)/shard_map/all_to_all | solution.py:445
  143.7 48.3 %copy-start.3 = (bf16[256,16,128]{2,1,0:T(8,128)(2,1)S(1)}, bf16[256,16,128]{2,1,0:T(8,128)(2,1)}, u32[]{:S(2)}) copy-start(bf16[256,16,128]{2,1,0:T(8,128)(2,1)} %get-tuple-element.29) | copy-start | bytes 3145732
  143.7 26.4 %collective-permute-start.3 = (bf16[8,32,16,128]{3,2,1,0:T(8,128)(2,1)}, bf16[8,32,16,128]{3,2,1,0:T(8,128)(2,1)}, u32[]{:S(2)}, u32[]{:S(2)}) collective-permute-start(bf16[8,32,16,128]{3,2,1,0:T(8,128)(2,1)} %bitcast.22), channel_id=1, source_target_pairs={{0,2},{2,0},{1,3},{3,1},{4,6},{6,4},{5,7},{7,5},{8,10},{10,8},{9,1... | collective-permute-start | bytes 3145736 | tf_op jit(solution)/shard_map/ppermute | solution.py:440
  144.8 47.2 %collective-permute-start.2 = (bf16[8,32,16,128]{3,2,1,0:T(8,128)(2,1)}, bf16[8,32,16,128]{3,2,1,0:T(8,128)(2,1)}, u32[]{:S(2)}, u32[]{:S(2)}) collective-permute-start(bf16[8,32,16,128]{3,2,1,0:T(8,128)(2,1)} %bitcast.21), channel_id=1, source_target_pairs={{0,2},{2,0},{1,3},{3,1},{4,6},{6,4},{5,7},{7,5},{8,10},{10,8},{9,1... | collective-permute-start | bytes 3145736 | tf_op jit(solution)/shard_map/ppermute | solution.py:440
  195.0 4.9 %copy-start.4 = (s32[192]{0:T(256)S(1)}, s32[192]{0:T(256)}, u32[]{:S(2)}) copy-start(s32[192]{0:T(256)} %refs_1_.7) | copy-start | bytes 2308
  195.0 7.4 %copy-start.1 = (bf16[8,32,32,128]{3,2,1,0:T(8,128)(2,1)}, bf16[8,32,32,128]{3,2,1,0:T(8,128)(2,1)S(1)}, u32[]{:S(2)}) copy-start(bf16[8,32,32,128]{3,2,1,0:T(8,128)(2,1)S(1)} %all-to-all-done.2.refs_3_) | copy-start | bytes 6291460
  195.0 42.8 %all-to-all-start.3 = ((bf16[8,24,32,128]{3,2,1,0:T(8,128)(2,1)}), bf16[8,24,32,128]{3,2,1,0:T(8,128)(2,1)}, u32[]{:S(2)}, u32[]{:S(2)}) async-start(bf16[8,24,32,128]{3,2,1,0:T(8,128)(2,1)} %pad_maximum_fusion), calls=%async_computation.3 | async-start | bytes 3145728 | tf_op jit(solution)/shard_map/all_to_all | solution.py:445
  237.8 18.8 %all-to-all-start.4 = ((bf16[8,8,32,128]{3,2,1,0:T(8,128)(2,1)}), bf16[8,8,32,128]{3,2,1,0:T(8,128)(2,1)S(1)}, u32[]{:S(2)}, u32[]{:S(2)}) async-start(bf16[8,8,32,128]{3,2,1,0:T(8,128)(2,1)} %pad_maximum_fusion.1), calls=%async_computation.4 | async-start | bytes 1048576 | tf_op jit(solution)/shard_map/all_to_all | solution.py:445
  256.6 0.8 copy-start.2

commit v5 on v4

--- a/solution.py
+++ b/solution.py
@@ -226,11 +226,14 @@
         lax.fori_loop(0, count // 8, some, 0)
 
     if owners:
-        own = out_refs[0].shape[0] // (owners // BLOCKS)
-        for way in range(owners // BLOCKS):
+        ways = owners // BLOCKS
+        own = out_refs[0].shape[0] // ways
+        for way in range(ways):
             for other in range(BLOCKS):
+                chip = lax.rem(place_ref[1 + 2 * other] + way // cores, ways // cores)
+                core = lax.rem(place_ref[2 + 2 * other] + way % cores, cores)
                 target = lax.rem(block + other, BLOCKS)
-                begin = ((way // cores * BLOCKS + target) * cores + way % cores) * own
+                begin = ((chip * BLOCKS + target) * cores + core) * own
                 corners(out_refs[other], begin, way * own, own)
     else:
         corners(out_refs[0], 0, 0, slots)
@@ -275,14 +278,18 @@
             pltpu.SemaphoreType.DMA,
         ],
         compiler_params=pltpu.CompilerParams(vmem_limit_bytes=VMEM_BYTES),
-        cost_estimate=pl.CostEstimate(flops=8 * flops, bytes_accessed=12 * 2**20, transcendentals=0),
+        cost_estimate=pl.CostEstimate(flops=6 * flops, bytes_accessed=12 * 2**20, transcendentals=0),
         name="filter_transform",
     )(place, spec_good, flags, voltages, coefs, table, voltages if after is None else after)
 
 
-def correlate_kernel(chips, cores, pieces, *refs):
-    scale_ref, refs = refs[0], refs[1:]
-    part_refs = refs[:pieces]
+def correlate_kernel(chips, cores, kinds, *refs):
+    scale_ref, place_ref, *refs = refs
+    part_refs = []
+    for by_way in kinds:
+        count = chips * cores if by_way else 1
+        part_refs.append(refs[:count])
+        refs = refs[count:]
     out_ref, straight, turned = refs[-3:]
     ins = LANES // cores
     total = straight.shape[1]
@@ -291,24 +298,31 @@
     upper = lax.broadcasted_iota(jnp.int32, (half, half), 1) >= lax.broadcasted_iota(jnp.int32, (half, half), 0)
 
     def one_slot(slot, carry):
-        for chip in range(chips):
-            lanes = pl.ds(chip * LANES, LANES)
-            place = 0
-            for part in part_refs:
-                columns = part.shape[0] // (chips * cores)
-                depth = part.shape[2]
-                half_depth = depth // 2
-                low = lax.broadcasted_iota(jnp.int32, (depth, LANES), 1) < ins
-                for column in range(columns):
-                    sources = [(chip * columns + column) * cores + core for core in range(cores)]
-                    one, two = (part[source, slot].astype(jnp.float32) for source in sources)
+        place = 0
+        for by_way, part in zip(kinds, part_refs):
+            depth = part[0].shape[-2]
+            half_depth = depth // 2
+            low = lax.broadcasted_iota(jnp.int32, (depth, LANES), 1) < ins
+            columns = 1 if by_way else part[0].shape[0] // (chips * cores)
+            for column in range(columns):
+                for step in range(chips):
+                    if by_way:
+                        chip = lax.rem(place_ref[0] + chips - step, chips)
+                        same, cross = (part[step * cores + core][slot].astype(jnp.float32) for core in range(cores))
+                        one = jnp.where(place_ref[1] == 0, same, cross)
+                        two = jnp.where(place_ref[1] == 0, cross, same)
+                    else:
+                        chip = step
+                        sources = [(chip * columns + column) * cores + core for core in range(cores)]
+                        one, two = (part[0][source, slot].astype(jnp.float32) for source in sources)
+                    lanes = pl.ds(pl.multiple_of(chip * LANES, LANES), LANES) if by_way else pl.ds(chip * LANES, LANES)
                     first = jnp.where(low, one, pltpu.roll(two, ins, 1))
                     second = jnp.where(low, pltpu.roll(one, ins, 1), two)
-                    for both in (first, second):
-                        rows = pl.ds(place, depth)
+                    for index, both in enumerate((first, second)):
+                        rows = pl.ds(place + index * depth, depth)
                         straight[rows, lanes] = both.astype(jnp.bfloat16)
                         turned[rows, lanes] = jnp.concatenate([-both[half_depth:], both[:half_depth]], axis=0).astype(jnp.bfloat16)
-                        place += depth
+                place += 2 * depth
         left = straight[...].T
 
         def product(a, ref, b):
@@ -325,19 +339,26 @@
     lax.fori_loop(0, out_ref.shape[0], one_slot, 0, unroll=2)
 
 
-def correlate(scale, parts, into, first, own, chips, cores):
-    count = min(part.shape[1] - begin for part, begin in parts)
+def correlate(scale, spot, parts, into, first, count, own, chips, cores):
     total = chips * LANES
-    depth = sum(part.shape[0] // chips * part.shape[2] for part, _ in parts)
-
-    def spec(part, begin):
-        return pl.BlockSpec((part.shape[0], SLOTS) + part.shape[2:], lambda c: (0, c + begin // SLOTS, 0, 0))
-
-    arrays = [part for part, _ in parts]
-    in_specs = [pl.BlockSpec(memory_space=pltpu.SMEM)] + [spec(*pair) for pair in parts]
-    operands = [scale] + arrays
+    arrays, in_specs, kinds, depth = [], [], [], 0
+    for part, begin in parts:
+        kinds.append(isinstance(part, list))
+        for array in part if kinds[-1] else [part]:
+            lead = () if kinds[-1] else (array.shape[0],)
+            tail = array.shape[-2:]
+            arrays.append(array)
+            at = begin // SLOTS
+            if lead:
+                in_specs.append(pl.BlockSpec(lead + (SLOTS,) + tail, lambda c, at=at: (0, c + at, 0, 0)))
+            else:
+                in_specs.append(pl.BlockSpec((SLOTS,) + tail, lambda c, at=at: (c + at, 0, 0)))
+        depth += cores * array.shape[-2] * (1 if kinds[-1] else array.shape[0] // (chips * cores))
+    smem = pl.BlockSpec(memory_space=pltpu.SMEM)
+    in_specs = [smem, smem] + in_specs
+    operands = [scale, spot] + arrays
     aliases = {}
-    kernel = functools.partial(correlate_kernel, chips, cores, len(parts))
+    kernel = functools.partial(correlate_kernel, chips, cores, tuple(kinds))
     if into is not None:
         aliases = {len(operands): 0}
         operands.append(into)
@@ -433,8 +454,12 @@
     scale = (1.0 / jnp.sum(spec_good).astype(jnp.float32)).reshape(1)
     next_flags = passed_along(input_flags[:, :taps], "tblk", -1)
 
-    def chunk(row_first, rows, table, after, flags=input_flags, **rest):
-        return transform(block.reshape(1), spec_good, flags, voltages, pfb_coeffs, table, after, row_first, rows, **rest)
+    spot = jnp.stack([lax.axis_index("inp"), lax.axis_index("sub")]).astype(jnp.int32)
+    start = jnp.zeros((2,), jnp.int32)
+
+    def chunk(row_first, rows, table, after, flags=input_flags, begin=(start, start), **rest):
+        place = jnp.concatenate([block.reshape(1), *begin])
+        return transform(place, spec_good, flags, voltages, pfb_coeffs, table, after, row_first, rows, **rest)
 
     def swapped(piece):
         return lax.ppermute(piece, "tblk", [(0, 1), (1, 0)])
@@ -445,40 +470,61 @@
         return lax.all_to_all(piece, axes, split_axis=0, concat_axis=0, tiled=True), before
 
     column = ("inp", "sub")
+
+    def sent(way, piece):
+        if way == 0:
+            return piece
+        step, other = way // cores, way % cores
+        pairs = [
+            (chip * cores + core, (chip + step) % chips * cores + (core + other) % cores)
+            for chip in range(chips)
+            for core in range(cores)
+        ]
+        return lax.ppermute(piece, column, pairs)
+
+    order = sorted(range(ways), key=lambda way: (-min(way // cores, chips - way // cores), way))
+
+    def spread(pieces):
+        came = {way: sent(way, pieces(way)) for way in order}
+        return [came[way] for way in range(ways)]
+
     table, early = chunk(STEP, STEP, chan_map.reshape(slots, 1), None)
     early = early.reshape(owners, own, *early.shape[1:])
     early, _ = turn(early, ("inp", "tblk", "sub"), None)
     split = dict(owners=owners, cores=cores)
-    middle = [part.reshape(ways, own, *part.shape[1:]) for part in chunk(2 * STEP, 2 * STEP, table, table, **split)]
+    middle = [part.reshape(ways, own, *part.shape[1:]) for part in chunk(2 * STEP, 2 * STEP, table, table, begin=(start, start), **split)]
     middle_own, early = turn(middle[0], column, early)
     middle_other = swapped(middle[1])
-    over = [part.reshape(ways, own, *part.shape[1:]) for part in chunk(0, STEP, table, middle[0], next_flags, nexts=True, **split)]
-    late = [part.reshape(ways, own, *part.shape[1:]) for part in chunk(0, STEP, table, over[0], **split)]
-    late_other, over_other = swapped(late[1]), swapped(over[1])
+    over = [part.reshape(ways, own, *part.shape[1:]) for part in chunk(0, STEP, table, middle[0], next_flags, begin=(spot, spot), nexts=True, **split)]
+    late = [part.reshape(ways, own, *part.shape[1:]) for part in chunk(0, STEP, table, over[0], begin=(spot, spot), **split)]
+    groups = [(0, own // 2), (own // 2, own)]
+    whole = [swapped(part[1]) for part in (late, over)]
+    others = [[part[:, begin:end] for part in whole] for begin, end in groups]
     middle_other, late[0] = lax.optimization_barrier((middle_other, late[0]))
     middle_other, middle_own = turn(middle_other, column, middle_own)
 
+    (late, over, middle_own) = lax.optimization_barrier((late, over, middle_own))
+
     def added(a, b, here):
         return (a.astype(jnp.float32) + jnp.where(here, b.astype(jnp.float32), 0.0)).astype(jnp.bfloat16)
 
-    out, before = None, middle_other
-    cut = own * 3 // 4
-    tails = []
-    for begin, end in ((0, cut), (cut, own)):
-        mine = added(late[0][:, begin:end], over_other[:, begin:end], block > 0)
-        others = added(late_other[:, begin:end], over[0][:, begin:end], block == 0)
-        half = mine.shape[2] // 2
-        piece = jnp.concatenate([mine[:, :, :half], others[:, :, :half], mine[:, :, half:], others[:, :, half:]], axis=2)
-        tail, before = turn(piece, column, before)
-        if tails:
-            tails[0] = before
-        else:
-            middle_other = before
-        tails.append(tail)
-        before = tail
-    for (begin, end), tail in zip(((0, cut), (cut, own)), tails):
+    out = None
+    for (begin, end), (late_other, over_other) in zip(groups, others):
+
+        def piece(way):
+            mine = added(late[0][way, begin:end], over_other[way], block > 0)
+            other = added(late_other[way], over[0][way, begin:end], block == 0)
+            half = mine.shape[1] // 2
+            return jnp.concatenate([mine[:, :half], other[:, :half], mine[:, half:], other[:, half:]], axis=1)
+
+        tail = spread(piece)
+        if end < own:
+            came = [tail[way] for way in order[:4]]
+            late, over, came = lax.optimization_barrier((late, over, came))
+            for way, part in zip(order, came):
+                tail[way] = part
         parts = [(early, begin), (middle_own, begin), (middle_other, begin), (tail, 0)]
-        out = correlate(scale, parts, out, begin, own, chips, cores)
+        out = correlate(scale, spot, parts, out, begin, end - begin, own, chips, cores)
     return out
 
 

time: 265 us -> 251 us (0.947)
  waiting for transfers between devices: 88.2 us -> 58.8 us
  Pallas kernels: 118 us -> 126 us
  local copies, waits for them, and re-layouts: 4.76 us -> 8.97 us
    all_to_all x5 -> x3, waiting for transfers between devices: 43.8 us -> 5.46 us  [turn(): lax.all_to_all(piece, axes, split_axis=0, concat_axis=0, tiled=True)]
    ppermute x0 -> x14, waiting for transfers between devices: none -> 26.7 us  [sent(): return lax.ppermute(piece, column, pairs)]
    ppermute x3, waiting for transfers between devices: 44.3 us -> 26.6 us  [swapped(): return lax.ppermute(piece, 'tblk', [(0, 1), (1, 0)])]
    ppermute x0 -> x14, starting transfers between devices: none -> 17.1 us  [sent(): return lax.ppermute(piece, column, pairs)]
    ppermute x3, starting transfers between devices: 13.3 us -> 2.43 us  [swapped(): return lax.ppermute(piece, 'tblk', [(0, 1), (1, 0)])]
    pallas_call x4, Pallas kernels: 98.2 us -> 106 us  [transform(): pl.pallas_call(functools.partial(transform_kernel, row_first, rows, nexts...]
    all_to_all x5 -> x3, starting transfers between devices: 28.8 us -> 23.6 us  [turn(): lax.all_to_all(piece, axes, split_axis=0, concat_axis=0, tiled=True)]
    unnamed x12 -> x38, local copies, waits for them, and re-layouts: 2.72 us -> 6.02 us
  transfers between devices with their start and end apart: 9 -> 21, of which waited for: 5 -> 6; matrix products, arithmetic and copies ran while one was open for 4% -> 4% of each run, Pallas kernels for 43% -> 47%
where the time goes in v5:
time: 251 us; the launch traced here: 247 us
  Pallas kernels  126 us (50%)
  waiting for transfers between devices  58.8 us (23%)
  starting transfers between devices  44.4 us (18%)
  local copies, waits for them, and re-layouts  8.97 us (4%)
  other arithmetic  7.49 us (3%)
    pallas_call x4, Pallas kernels, transform(): pl.pallas_call(functools.partial(transform_kernel, row_first, rows, nexts...  106 us
    ppermute x14, waiting for transfers between devices, sent(): return lax.ppermute(piece, column, pairs)  26.7 us
    ppermute x3, waiting for transfers between devices, swapped(): return lax.ppermute(piece, 'tblk', [(0, 1), (1, 0)])  26.6 us
    all_to_all x3, starting transfers between devices, turn(): lax.all_to_all(piece, axes, split_axis=0, concat_axis=0, tiled=True)  23.6 us
    pallas_call x2, Pallas kernels, correlate(): pl.pallas_call(kernel, grid=(count // SLOTS,), out_shape=jax.ShapeDtypeSt...  20.7 us
    ppermute x14, starting transfers between devices, sent(): return lax.ppermute(piece, column, pairs)  17.1 us
    unnamed x38, local copies, waits for them, and re-layouts  6.02 us
    all_to_all x3, waiting for transfers between devices, turn(): lax.all_to_all(piece, axes, split_axis=0, concat_axis=0, tiled=True)  5.46 us
  transfers between devices with their start and end apart: 21, of which 6 were waited for; matrix products, arithmetic and copies ran while one was open for 4% of the time, Pallas kernels for 47%

profile of v5, /device:TPU:0, one launch (start us, length us, event | category | flops | bytes accessed | tf_op | source)
XLA Modules:
  0.0 247.1 jit_solution(6562629624757601288)
XLA Ops:
  0.0 1.3 collective-permute-start.1
  1.3 1.5 copy.7.refs_5_
  3.3 26.2 %filter_transform.4 = (bf16[1024,2048]{1,0:T(8,128)(2,1)}, bf16[512,16,128]{2,1,0:T(8,128)(2,1)}) custom-call(s32[5]{0:T(128)} %concatenate.58.refs_0_, s32[192]{0:T(256)} %refs_1_.7, s32[64,96]{1,0:T(8,128)} %refs_2_.5, bf16[64,196608]{1,0:T(8,128)(2,1)} %refs_3_.7, f32[16,2048]{1,0:T(8,128)} %refs_4_.7, s32[512,1]{1,0:T(8,128)} %copy.7.refs_5_, ...), custom_call_target="tpu_custom_call" | custom-call | flops 25769803776 | bytes 12582912 | tf_op jit(solution)/shard_map/filter_transform/pallas_call | solution.py:263
  29.6 9.4 %all-to-all-start = ((bf16[16,32,16,128]{3,2,1,0:T(8,128)(2,1)}), bf16[16,32,16,128]{3,2,1,0:T(8,128)(2,1)S(1)}, u32[]{:S(2)}, u32[]{:S(2)}) async-start(bf16[16,32,16,128]{3,2,1,0:T(8,128)(2,1)} %bitcast.79), calls=%async_computation | async-start | bytes 4194304 | tf_op jit(solution)/shard_map/all_to_all | solution.py:470
  39.0 40.6 %filter_transform.5 = (bf16[256,32,128]{2,1,0:T(8,128)(2,1)}, bf16[256,32,128]{2,1,0:T(8,128)(2,1)}) custom-call(s32[5]{0:T(128)} %concatenate.58.refs_0_, s32[192]{0:T(256)} %refs_1_.7, s32[64,96]{1,0:T(8,128)} %refs_2_.5, bf16[64,196608]{1,0:T(8,128)(2,1)} %refs_3_.7, f32[16,2048]{1,0:T(8,128)} %refs_4_.7, ...), custom_call_target="tpu_custom_call" | custom-call | flops 51539607552 | bytes 12582912 | tf_op jit(solution)/shard_map/filter_transform/pallas_call | solution.py:263
  80.3 1.3 copy-done
  81.6 10.6 %all-to-all-start.1 = ((bf16[8,32,32,128]{3,2,1,0:T(8,128)(2,1)}), bf16[8,32,32,128]{3,2,1,0:T(8,128)(2,1)}, u32[]{:S(2)}, u32[]{:S(2)}) async-start(bf16[8,32,32,128]{3,2,1,0:T(8,128)(2,1)} %bitcast.77), calls=%async_computation.1 | async-start | bytes 4194304 | tf_op jit(solution)/shard_map/all_to_all | solution.py:470
  92.8 17.8 %filter_transform.6 = (bf16[256,16,128]{2,1,0:T(8,128)(2,1)}, bf16[256,16,128]{2,1,0:T(8,128)(2,1)}) custom-call(s32[5]{0:T(128)} %concatenate.59.refs_0_, s32[192]{0:T(256)} %refs_1_.7, s32[64,16]{1,0:T(8,128)} %copy-done.18, bf16[64,196608]{1,0:T(8,128)(2,1)} %refs_3_.7, f32[16,2048]{1,0:T(8,128)} %refs_4_.7, ...), custom_call_target="tpu_custom_call" | custom-call | flops 25769803776 | bytes 12582912 | tf_op jit(solution)/shard_map/filter_transform/pallas_call | solution.py:263
  110.7 21.0 %filter_transform.7 = (bf16[256,16,128]{2,1,0:T(8,128)(2,1)}, bf16[256,16,128]{2,1,0:T(8,128)(2,1)}) custom-call(s32[5]{0:T(128)} %concatenate.59.refs_0_, s32[192]{0:T(256)} %refs_1_.7, s32[64,96]{1,0:T(8,128)} %refs_2_.5, bf16[64,196608]{1,0:T(8,128)(2,1)} %refs_3_.7, f32[16,2048]{1,0:T(8,128)} %refs_4_.7, ...), custom_call_target="tpu_custom_call" | custom-call | flops 25769803776 | bytes 12582912 | tf_op jit(solution)/shard_map/filter_transform/pallas_call | solution.py:263
  131.7 2.3 collective-permute-start.3
  135.9 5.5 %all-to-all-done.1.refs_3_ = bf16[8,32,32,128]{3,2,1,0:T(8,128)(2,1)} async-done(((bf16[8,32,32,128]{3,2,1,0:T(8,128)(2,1)}), bf16[8,32,32,128]{3,2,1,0:T(8,128)(2,1)}, u32[]{:S(2)}, u32[]{:S(2)}) %all-to-all-start.1) | async-done | bytes 2097184 | tf_op jit(solution)/shard_map/all_to_all | solution.py:470
  141.4 3.6 %all-to-all-start.2 = ((bf16[8,32,32,128]{3,2,1,0:T(8,128)(2,1)}), bf16[8,32,32,128]{3,2,1,0:T(8,128)(2,1)S(1)}, u32[]{:S(2)}, u32[]{:S(2)}) async-start(bf16[8,32,32,128]{3,2,1,0:T(8,128)(2,1)} %collective-permute-done), calls=%async_computation.2 | async-start | bytes 4194304 | tf_op jit(solution)/shard_map/all_to_all | solution.py:470
  145.0 5.8 %collective-permute-done.2 = bf16[8,32,16,128]{3,2,1,0:T(8,128)(2,1)S(1)} collective-permute-done((bf16[8,32,16,128]{3,2,1,0:T(8,128)(2,1)}, bf16[8,32,16,128]{3,2,1,0:T(8,128)(2,1)S(1)}, u32[]{:S(2)}, u32[]{:S(2)}) %collective-permute-start.2) | collective-permute-done | bytes 1048608 | tf_op jit(solution)/shard_map/ppermute | solution.py:465
  150.8 1.2 fusion.30
  152.0 20.8 %collective-permute-done.3 = bf16[8,32,16,128]{3,2,1,0:T(8,128)(2,1)} collective-permute-done((bf16[8,32,16,128]{3,2,1,0:T(8,128)(2,1)}, bf16[8,32,16,128]{3,2,1,0:T(8,128)(2,1)}, u32[]{:S(2)}, u32[]{:S(2)}) %collective-permute-start.3) | collective-permute-done | bytes 1048608 | tf_op jit(solution)/shard_map/ppermute | solution.py:465
  172.9 1.2 fusion.31
  174.2 5.4 %collective-permute-start.4 = (bf16[16,32,128]{2,1,0:T(8,128)(2,1)S(1)}, bf16[16,32,128]{2,1,0:T(8,128)(2,1)S(1)}, u32[]{:S(2)}, u32[]{:S(2)}) collective-permute-start(bf16[16,32,128]{2,1,0:T(8,128)(2,1)S(1)} %pad_maximum_fusion), channel_id=1, source_target_pairs={{0,8},{1,9},{4,12},{5,13},{8,0},{9,1},{12,4},{13,5},{2,10},{3,11},... | collective-permute-start | bytes 393224 | tf_op jit(solution)/shard_map/ppermute | solution.py:483
  179.8 0.8 collective-permute-start.6
  180.7 2.2 collective-permute-start.7
  183.2 0.7 pad_maximum_fusion.12.refs_5_
  183.8 24.6 %collective-permute-done.4.refs_9_ = bf16[16,32,128]{2,1,0:T(8,128)(2,1)S(1)} collective-permute-done((bf16[16,32,128]{2,1,0:T(8,128)(2,1)S(1)}, bf16[16,32,128]{2,1,0:T(8,128)(2,1)S(1)}, u32[]{:S(2)}, u32[]{:S(2)}) %collective-permute-start.4) | collective-permute-done | bytes 131104 | tf_op jit(solution)/shard_map/ppermute | solution.py:483
  208.5 1.9 collective-permute-done.5.refs_10_
  211.7 1.2 fusion.23
  213.2 0.8 collective-permute-start.8
  214.0 1.1 collective-permute-start.9
  215.4 0.7 pad_maximum_fusion.7
  216.1 0.7 pad_maximum_fusion.4.refs_5_
  216.9 2.6 %collective-permute-start.11 = (bf16[16,32,128]{2,1,0:T(8,128)(2,1)S(1)}, bf16[16,32,128]{2,1,0:T(8,128)(2,1)S(1)}, u32[]{:S(2)}, u32[]{:S(2)}) collective-permute-start(bf16[16,32,128]{2,1,0:T(8,128)(2,1)S(1)} %pad_maximum_fusion.8), channel_id=1, source_target_pairs={{0,8},{1,9},{4,12},{5,13},{8,0},{9,1},{12,4},{13,5},{2,10},{3,11},... | collective-permute-start | bytes 393224 | tf_op jit(solution)/shard_map/ppermute | solution.py:483
  220.0 3.0 %collective-permute-start.13 = (bf16[16,32,128]{2,1,0:T(8,128)(2,1)S(1)}, bf16[16,32,128]{2,1,0:T(8,128)(2,1)S(1)}, u32[]{:S(2)}, u32[]{:S(2)}) collective-permute-start(bf16[16,32,128]{2,1,0:T(8,128)(2,1)S(1)} %pad_maximum_fusion.10), channel_id=1, source_target_pairs={{0,12},{1,13},{4,0},{5,1},{8,4},{9,5},{12,8},{13,9},{2,14},{3,15},... | collective-permute-start | bytes 393224 | tf_op jit(solution)/shard_map/ppermute | solution.py:483
  223.4 1.4 copy-done.1
  224.8 10.3 %correlate.2.refs_13_ = bf16[32,512,512]{2,1,0:T(8,128)(2,1)} custom-call(f32[1]{0:T(128)} %bitcast.refs_0_, s32[2]{0:T(128)} %pad_add_fusion.refs_1_, bf16[16,32,16,128]{3,2,1,0:T(8,128)(2,1)} %copy-done, bf16[8,32,32,128]{3,2,1,0:T(8,128)(2,1)} %all-to-all-done.1.refs_3_, bf16[8,32,32,128]{3,2,1,0:T(8,128)(2,1)} %copy-done.1, ...), custom_call_target="tpu_custom_call" | custom-call | flops 8589934592 | bytes 12582912 | tf_op jit(solution)/shard_map/correlate/pallas_call | solution.py:366
  236.8 10.4 %correlate.3 = bf16[32,512,512]{2,1,0:T(8,128)(2,1)} custom-call(f32[1]{0:T(128)} %bitcast.refs_0_, s32[2]{0:T(128)} %pad_add_fusion.refs_1_, bf16[16,32,16,128]{3,2,1,0:T(8,128)(2,1)} %copy-done, bf16[8,32,32,128]{3,2,1,0:T(8,128)(2,1)} %all-to-all-done.1.refs_3_, bf16[8,32,32,128]{3,2,1,0:T(8,128)(2,1)} %copy-done.1, ...), custom_call_target="tpu_custom_call", output_to_operand_aliasing={{}: (13, {})} | custom-call | flops 8589934592 | bytes 12582912 | tf_op jit(solution)/shard_map/correlate/pallas_call | solution.py:366
  (103 shorter events, 8.0 us)
Async XLA Ops:
  0.0 92.2 %collective-permute-start.1 = (s32[64,16]{1,0:T(8,128)}, s32[64,16]{1,0:T(8,128)S(1)}, u32[]{:S(2)}, u32[]{:S(2)}) collective-permute-start(s32[64,16]{1,0:T(8,128)} %bitcast.89), channel_id=1, source_target_pairs={{2,0},{3,1},{6,4},{7,5},{10,8},{11,9},{14,12},{15,13},{18,16},{19,... | collective-permute-start | bytes 12296 | tf_op jit(solution)/shard_map/ppermute | solution.py:25
  29.6 50.7 %all-to-all-start = ((bf16[16,32,16,128]{3,2,1,0:T(8,128)(2,1)}), bf16[16,32,16,128]{3,2,1,0:T(8,128)(2,1)S(1)}, u32[]{:S(2)}, u32[]{:S(2)}) async-start(bf16[16,32,16,128]{3,2,1,0:T(8,128)(2,1)} %bitcast.79), calls=%async_computation | async-start | bytes 4194304 | tf_op jit(solution)/shard_map/all_to_all | solution.py:470
  79.6 56.3 %collective-permute-start = (bf16[8,32,32,128]{3,2,1,0:T(8,128)(2,1)}, bf16[8,32,32,128]{3,2,1,0:T(8,128)(2,1)}, u32[]{:S(2)}, u32[]{:S(2)}) collective-permute-start(bf16[8,32,32,128]{3,2,1,0:T(8,128)(2,1)} %bitcast.86), channel_id=1, source_target_pairs={{0,2},{2,0},{1,3},{3,1},{4,6},{6,4},{5,7},{7,5},{8,10},{10,8},{9,1... | collective-permute-start | bytes 6291464 | tf_op jit(solution)/shard_map/ppermute | solution.py:465
  80.3 1.3 copy-start
  81.6 59.7 %all-to-all-start.1 = ((bf16[8,32,32,128]{3,2,1,0:T(8,128)(2,1)}), bf16[8,32,32,128]{3,2,1,0:T(8,128)(2,1)}, u32[]{:S(2)}, u32[]{:S(2)}) async-start(bf16[8,32,32,128]{3,2,1,0:T(8,128)(2,1)} %bitcast.77), calls=%async_computation.1 | async-start | bytes 4194304 | tf_op jit(solution)/shard_map/all_to_all | solution.py:470
  110.6 40.2 %collective-permute-start.2 = (bf16[8,32,16,128]{3,2,1,0:T(8,128)(2,1)}, bf16[8,32,16,128]{3,2,1,0:T(8,128)(2,1)S(1)}, u32[]{:S(2)}, u32[]{:S(2)}) collective-permute-start(bf16[8,32,16,128]{3,2,1,0:T(8,128)(2,1)} %bitcast.88), channel_id=1, source_target_pairs={{0,2},{2,0},{1,3},{3,1},{4,6},{6,4},{5,7},{7,5},{8,10},{10,8},{9,1... | collective-permute-start | bytes 3145736 | tf_op jit(solution)/shard_map/ppermute | solution.py:465
  110.6 23.3 %copy-start.11 = (s32[192]{0:T(256)S(1)}, s32[192]{0:T(256)}, u32[]{:S(2)}) copy-start(s32[192]{0:T(256)} %refs_1_.7) | copy-start | bytes 2308
  131.7 41.2 %collective-permute-start.3 = (bf16[8,32,16,128]{3,2,1,0:T(8,128)(2,1)}, bf16[8,32,16,128]{3,2,1,0:T(8,128)(2,1)}, u32[]{:S(2)}, u32[]{:S(2)}) collective-permute-start(bf16[8,32,16,128]{3,2,1,0:T(8,128)(2,1)} %bitcast.87), channel_id=1, source_target_pairs={{0,2},{2,0},{1,3},{3,1},{4,6},{6,4},{5,7},{7,5},{8,10},{10,8},{9,1... | collective-permute-start | bytes 3145736 | tf_op jit(solution)/shard_map/ppermute | solution.py:465
  141.4 82.1 %all-to-all-start.2 = ((bf16[8,32,32,128]{3,2,1,0:T(8,128)(2,1)}), bf16[8,32,32,128]{3,2,1,0:T(8,128)(2,1)S(1)}, u32[]{:S(2)}, u32[]{:S(2)}) async-start(bf16[8,32,32,128]{3,2,1,0:T(8,128)(2,1)} %collective-permute-done), calls=%async_computation.2 | async-start | bytes 4194304 | tf_op jit(solution)/shard_map/all_to_all | solution.py:470
  145.0 27.9 %copy-start.3 = (bf16[256,16,128]{2,1,0:T(8,128)(2,1)S(1)}, bf16[256,16,128]{2,1,0:T(8,128)(2,1)}, u32[]{:S(2)}) copy-start(bf16[256,16,128]{2,1,0:T(8,128)(2,1)} %get-tuple-element.33) | copy-start | bytes 3145732
  174.2 34.3 %collective-permute-start.4 = (bf16[16,32,128]{2,1,0:T(8,128)(2,1)S(1)}, bf16[16,32,128]{2,1,0:T(8,128)(2,1)S(1)}, u32[]{:S(2)}, u32[]{:S(2)}) collective-permute-start(bf16[16,32,128]{2,1,0:T(8,128)(2,1)S(1)} %pad_maximum_fusion), channel_id=1, source_target_pairs={{0,8},{1,9},{4,12},{5,13},{8,0},{9,1},{12,4},{13,5},{2,10},{3,11},... | collective-permute-start | bytes 393224 | tf_op jit(solution)/shard_map/ppermute | solution.py:483
  179.6 30.7 %collective-permute-start.5 = (bf16[16,32,128]{2,1,0:T(8,128)(2,1)S(1)}, bf16[16,32,128]{2,1,0:T(8,128)(2,1)S(1)}, u32[]{:S(2)}, u32[]{:S(2)}) collective-permute-start(bf16[16,32,128]{2,1,0:T(8,128)(2,1)S(1)} %pad_maximum_fusion.1), channel_id=1, source_target_pairs={{0,9},{1,8},{4,13},{5,12},{8,1},{9,0},{12,5},{13,4},{2,11},{3,10},... | collective-permute-start | bytes 393224 | tf_op jit(solution)/shard_map/ppermute | solution.py:483
  179.8 30.5 %collective-permute-start.6 = (bf16[16,32,128]{2,1,0:T(8,128)(2,1)S(1)}, bf16[16,32,128]{2,1,0:T(8,128)(2,1)S(1)}, u32[]{:S(2)}, u32[]{:S(2)}) collective-permute-start(bf16[16,32,128]{2,1,0:T(8,128)(2,1)S(1)} %pad_maximum_fusion.2), channel_id=1, source_target_pairs={{0,4},{1,5},{4,8},{5,9},{8,12},{9,13},{12,0},{13,1},{2,6},{3,7},{6... | collective-permute-start | bytes 393224 | tf_op jit(solution)/shard_map/ppermute | solution.py:483
  180.6 32.3 %copy-start.2 = (bf16[256,16,128]{2,1,0:T(8,128)(2,1)S(1)}, bf16[256,16,128]{2,1,0:T(8,128)(2,1)}, u32[]{:S(2)}) copy-start(bf16[256,16,128]{2,1,0:T(8,128)(2,1)} %get-tuple-element.34) | copy-start | bytes 3145732
  180.7 31.0 %collective-permute-start.7 = (bf16[16,32,128]{2,1,0:T(8,128)(2,1)S(1)}, bf16[16,32,128]{2,1,0:T(8,128)(2,1)}, u32[]{:S(2)}, u32[]{:S(2)}) collective-permute-start(bf16[16,32,128]{2,1,0:T(8,128)(2,1)S(1)} %pad_maximum_fusion.3), channel_id=1, source_target_pairs={{0,5},{1,4},{4,9},{5,8},{8,13},{9,12},{12,1},{13,0},{2,7},{3,6},{6... | collective-permute-start | bytes 393224 | tf_op jit(solution)/shard_map/ppermute | solution.py:483
  182.9 33.8 %collective-permute-start.15 = (bf16[16,32,128]{2,1,0:T(8,128)(2,1)S(1)}, bf16[16,32,128]{2,1,0:T(8,128)(2,1)S(1)}, u32[]{:S(2)}, u32[]{:S(2)}) collective-permute-start(bf16[16,32,128]{2,1,0:T(8,128)(2,1)S(1)} %pad_maximum_fusion.13), channel_id=1, source_target_pairs={{0,1},{1,0},{4,5},{5,4},{8,9},{9,8},{12,13},{13,12},{2,3},{3,2},{6... | collective-permute-start | bytes 393224 | tf_op jit(solution)/shard_map/ppermute | solution.py:483
  208.5 1.9 copy-start.12
  208.5 8.4 %collective-permute-start.16 = (bf16[16,32,128]{2,1,0:T(8,128)(2,1)S(1)}, bf16[16,32,128]{2,1,0:T(8,128)(2,1)S(1)}, u32[]{:S(2)}, u32[]{:S(2)}) collective-permute-start(bf16[16,32,128]{2,1,0:T(8,128)(2,1)S(1)} %pad_maximum_fusion.14), channel_id=1, source_target_pairs={{0,12},{1,13},{4,0},{5,1},{8,4},{9,5},{12,8},{13,9},{2,14},{3,15},... | collective-permute-start | bytes 393224 | tf_op jit(solution)/shard_map/ppermute | solution.py:483
  210.3 9.2 %collective-permute-start.17 = (bf16[16,32,128]{2,1,0:T(8,128)(2,1)S(1)}, bf16[16,32,128]{2,1,0:T(8,128)(2,1)S(1)}, u32[]{:S(2)}, u32[]{:S(2)}) collective-permute-start(bf16[16,32,128]{2,1,0:T(8,128)(2,1)S(1)} %pad_maximum_fusion.15), channel_id=1, source_target_pairs={{0,13},{1,12},{4,1},{5,0},{8,5},{9,4},{12,9},{13,8},{2,15},{3,14},... | collective-permute-start | bytes 393224 | tf_op jit(solution)/shard_map/ppermute | solution.py:483
  213.2 6.8 %collective-permute-start.8 = (bf16[16,32,128]{2,1,0:T(8,128)(2,1)S(1)}, bf16[16,32,128]{2,1,0:T(8,128)(2,1)S(1)}, u32[]{:S(2)}, u32[]{:S(2)}) collective-permute-start(bf16[16,32,128]{2,1,0:T(8,128)(2,1)S(1)} %pad_maximum_fusion.5), channel_id=1, source_target_pairs={{0,1},{1,0},{4,5},{5,4},{8,9},{9,8},{12,13},{13,12},{2,3},{3,2},{6... | collective-permute-start | bytes 393224 | tf_op jit(solution)/shard_map/ppermute | solution.py:483
  214.0 8.9 %collective-permute-start.9 = (bf16[16,32,128]{2,1,0:T(8,128)(2,1)S(1)}, bf16[16,32,128]{2,1,0:T(8,128)(2,1)S(1)}, u32[]{:S(2)}, u32[]{:S(2)}) collective-permute-start(bf16[16,32,128]{2,1,0:T(8,128)(2,1)S(1)} %pad_maximum_fusion.6), channel_id=1, source_target_pairs={{0,4},{1,5},{4,8},{5,9},{8,12},{9,13},{12,0},{13,1},{2,6},{3,7},{6... | collective-permute-start | bytes 393224 | tf_op jit(solution)/shard_map/ppermute | solution.py:483
  216.8 6.2 %copy-start.15 = (bf16[16,32,128]{2,1,0:T(8,128)(2,1)}, bf16[16,32,128]{2,1,0:T(8,128)(2,1)S(1)}, u32[]{:S(2)}) copy-start(bf16[16,32,128]{2,1,0:T(8,128)(2,1)S(1)} %collective-permute-done.15.refs_6_) | copy-start | bytes 393220
  216.8 18.4 %collective-permute-start.10 = (bf16[16,32,128]{2,1,0:T(8,128)(2,1)}, bf16[16,32,128]{2,1,0:T(8,128)(2,1)S(1)}, u32[]{:S(2)}, u32[]{:S(2)}) collective-permute-start(bf16[16,32,128]{2,1,0:T(8,128)(2,1)} %pad_maximum_fusion.7), channel_id=1, source_target_pairs={{0,5},{1,4},{4,9},{5,8},{8,13},{9,12},{12,1},{13,0},{2,7},{3,6},{6... | collective-permute-start | bytes 393224 | tf_op jit(solution)/shard_map/ppermute | solution.py:483
  216.9 6.1 %copy-start.16 = (bf16[16,32,128]{2,1,0:T(8,128)(2,1)}, bf16[16,32,128]{2,1,0:T(8,128)(2,1)S(1)}, u32[]{:S(2)}) copy-start(bf16[16,32,128]{2,1,0:T(8,128)(2,1)S(1)} %collective-permute-done.16.refs_11_) | copy-start | bytes 393220
  216.9 18.3 %collective-permute-start.11 = (bf16[16,32,128]{2,1,0:T(8,128)(2,1)S(1)}, bf16[16,32,128]{2,1,0:T(8,128)(2,1)S(1)}, u32[]{:S(2)}, u32[]{:S(2)}) collective-permute-start(bf16[16,32,128]{2,1,0:T(8,128)(2,1)S(1)} %pad_maximum_fusion.8), channel_id=1, source_target_pairs={{0,8},{1,9},{4,12},{5,13},{8,0},{9,1},{12,4},{13,5},{2,10},{3,11},... | collective-permute-start | bytes 393224 | tf_op jit(solution)/shard_map/ppermute | solution.py:483
  219.5 3.5 %copy-start.17 = (bf16[16,32,128]{2,1,0:T(8,128)(2,1)}, bf16[16,32,128]{2,1,0:T(8,128)(2,1)S(1)}, u32[]{:S(2)}) copy-start(bf16[16,32,128]{2,1,0:T(8,128)(2,1)S(1)} %collective-permute-done.17.refs_12_) | copy-start | bytes 393220
  219.5 15.9 %collective-permute-start.12 = (bf16[16,32,128]{2,1,0:T(8,128)(2,1)S(1)}, bf16[16,32,128]{2,1,0:T(8,128)(2,1)S(1)}, u32[]{:S(2)}, u32[]{:S(2)}) collective-permute-start(bf16[16,32,128]{2,1,0:T(8,128)(2,1)S(1)} %pad_maximum_fusion.9), channel_id=1, source_target_pairs={{0,9},{1,8},{4,13},{5,12},{8,1},{9,0},{12,5},{13,4},{2,11},{3,10},... | collective-permute-start | bytes 393224 | tf_op jit(solution)/shard_map/ppermute | solution.py:483
  220.0 15.2 %copy-start.4 = (bf16[16,32,128]{2,1,0:T(8,128)(2,1)}, bf16[16,32,128]{2,1,0:T(8,128)(2,1)S(1)}, u32[]{:S(2)}) copy-start(bf16[16,32,128]{2,1,0:T(8,128)(2,1)S(1)} %collective-permute-done.8.refs_6_) | copy-start | bytes 393220
  220.0 15.4 %collective-permute-start.13 = (bf16[16,32,128]{2,1,0:T(8,128)(2,1)S(1)}, bf16[16,32,128]{2,1,0:T(8,128)(2,1)S(1)}, u32[]{:S(2)}, u32[]{:S(2)}) collective-permute-start(bf16[16,32,128]{2,1,0:T(8,128)(2,1)S(1)} %pad_maximum_fusion.10), channel_id=1, source_target_pairs={{0,12},{1,13},{4,0},{5,1},{8,4},{9,5},{12,8},{13,9},{2,14},{3,15},... | collective-permute-start | bytes 393224 | tf_op jit(solution)/shard_map/ppermute | solution.py:483
  223.0 12.2 %copy-start.5 = (bf16[16,32,128]{2,1,0:T(8,128)(2,1)}, bf16[16,32,128]{2,1,0:T(8,128)(2,1)S(1)}, u32[]{:S(2)}) copy-start(bf16[16,32,128]{2,1,0:T(8,128)(2,1)S(1)} %collective-permute-done.9.refs_7_) | copy-start | bytes 393220
  223.0 12.4 %collective-permute-start.14 = (bf16[16,32,128]{2,1,0:T(8,128)(2,1)S(1)}, bf16[16,32,128]{2,1,0:T(8,128)(2,1)S(1)}, u32[]{:S(2)}, u32[]{:S(2)}) collective-permute-start(bf16[16,32,128]{2,1,0:T(8,128)(2,1)S(1)} %pad_maximum_fusion.11), channel_id=1, source_target_pairs={{0,13},{1,12},{4,1},{5,0},{8,5},{9,4},{12,9},{13,8},{2,15},{3,14},... | collective-permute-start | bytes 393224 | tf_op jit(solution)/shard_map/ppermute | solution.py:483
  223.4 1.4 copy-start.1
  (8 other events, 5.3 us)
